TPU v7x, 32 devices: a whole 2x2x4 slice. The times are simulated.
32 devices in a mesh: groups: 2 (over y), dp: 4 (over z), mp: 2 (over x), teach: 2 (over core).
Axes of the slice: x: 2, y: 2, z: 4, core: 2. Of those that a mesh axis runs over, the one named last changes fastest.
Arguments:
- resid: bfloat16 [16, 256, 1280], P(('groups', 'dp', 'teach')), parts along dimension 0, may hold values from -6 to 6
- gain_mlp: float32 [1280], replicated, may hold values from 0.25 to 1.75
- gain_out: float32 [1280], replicated, may hold values from 0.25 to 1.75
- w_in: bfloat16 [1280, 5120], P(None, 'mp'), may hold values from -0.15625 to 0.15625
- w_out: bfloat16 [5120, 1280], P('mp'), may hold values from -0.078125 to 0.078125
- a_dino: bfloat16 [1280, 1536], P(None, 'mp'), may hold values from -0.15625 to 0.15625
- b_dino: bfloat16 [1536, 1536], P('mp')
- a_sig: bfloat16 [1280, 1152], P(None, 'mp'), may hold values from -0.15625 to 0.15625
- b_sig: bfloat16 [1152, 1152], P('mp')
- dino_feats: bfloat16 [16, 256, 1536], P('groups', ('dp', 'teach'), 'mp'), parts along dimension 0
- sig_feats: bfloat16 [16, 256, 1152], P('groups', ('dp', 'teach'), 'mp'), parts along dimension 0
- owner: int32 [16], P('groups'), parts along dimension 0, may hold values from 0 to 7, each once
Outputs:
- grad_w_in: float32 [2560, 5120], P(('groups', 'dp', 'teach'), 'mp'), parts along dimension 0
- grad_w_out: float32 [10240, 1280], P(('groups', 'mp'), ('dp', 'teach')), parts along dimension 0
- grad_a_dino: float32 [2560, 1536], P(('groups', 'dp', 'teach'), 'mp'), parts along dimension 0
- grad_b_dino: float32 [3072, 1536], P(('groups', 'mp'), ('dp', 'teach')), parts along dimension 0
- grad_a_sig: float32 [2560, 1152], P(('groups', 'dp', 'teach'), 'mp'), parts along dimension 0
- grad_b_sig: float32 [2304, 1152], P(('groups', 'mp'), ('dp', 'teach')), parts along dimension 0
There are 2 independent parts, one for each index of `groups`. A program takes and returns all parts, laid end to end along the dimension named above; an argument that names none is the same for every part. Nothing has to cross between parts.
Inputs may be any that keep to these rules, and one draw needn't show every extreme that they name: owner is a permutation of the images of a group.
All inputs are finite; a program needn't handle non-finite values.
Results may differ from a plain program's by a relative error of at most 0.022.
Values may be sent and summed in bfloat16 or wider, within the bound.
No kernel may reach another device: no remote copies, remote signals or barrier semaphores. Data moves between devices by JAX's collectives and lax.ppermute only.
A program may use at most 128 MiB of HBM per device.

v0:
```python
import math

import jax
import jax.numpy as jnp
from jax import lax
from jax.experimental import pallas as pl
from jax.experimental.pallas import tpu as pltpu
from jax.sharding import PartitionSpec as P

EPS = 1e-06
ROOT = math.sqrt(2.0 / math.pi)
CUBE = 0.044715


def layer_norm(values, gain):
    center = values - jnp.mean(values, axis=-1, keepdims=True)
    spread = jnp.mean(center * center, axis=-1, keepdims=True)
    return center * lax.rsqrt(spread + EPS) * gain


def norm_back(values, gain, upstream):
    center = values - jnp.mean(values, axis=-1, keepdims=True)
    recip = lax.rsqrt(jnp.mean(center * center, axis=-1, keepdims=True) + EPS)
    unit = center * recip
    scaled = upstream * gain
    return recip * (
        scaled
        - jnp.mean(scaled, axis=-1, keepdims=True)
        - unit * jnp.mean(scaled * unit, axis=-1, keepdims=True)
    )


def gelu_and_slope(values):
    square = values * values
    bend = jnp.tanh(ROOT * values * (1.0 + CUBE * square))
    half = 0.5 * (1.0 + bend)
    slope = half + 0.5 * values * (1.0 - bend * bend) * (ROOT * (1.0 + 3.0 * CUBE * square))
    return (values * half).astype(jnp.bfloat16), slope.astype(jnp.bfloat16)


def tiles(count, step=256):
    return [(at, min(at + step, count)) for at in range(0, count, step)]


def lanes(at, size):
    return pl.ds(pl.multiple_of(at * size, size), size)


def in_vmem(count):
    return [pl.BlockSpec(memory_space=pltpu.VMEM)] * count


def row_dot(left, right):
    return lax.dot_general(
        left, right, (((1,), (1,)), ((), ())), preferred_element_type=jnp.float32
    )


def over_rows(left, right):
    return lax.dot_general(
        left, right, (((0,), (0,)), ((), ())), preferred_element_type=jnp.float32
    )


def params(flops, nbytes, room=8):
    return dict(
        compiler_params=pltpu.CompilerParams(vmem_limit_bytes=room * 1024 * 1024),
        cost_estimate=pl.CostEstimate(flops=flops, bytes_accessed=nbytes, transcendentals=0),
    )


def mlp_forward(resid, gain, w_in, w_out):
    rows, width = resid.shape
    units = w_in.shape[1]
    steps = 2 if units % 256 == 0 else 1
    tile = units // steps
    step = next(c for c in (256, 128, tile) if tile % c == 0)
    wide = next(c for c in (256, 128, width) if width % c == 0)

    def kernel(resid_ref, gain_ref, w_in_hbm, w_out_hbm, normed_ref, hid_ref, slope_ref, out_ref, w_in_ref, w_out_ref, in_sem, out_sem):
        def into(at):
            cut = pl.ds(at * tile, tile)
            return pltpu.make_async_copy(w_in_hbm.at[:, cut], w_in_ref.at[:, cut], in_sem.at[at])

        def out_of(at):
            cut = pl.ds(at * tile, tile)
            return pltpu.make_async_copy(w_out_hbm.at[cut, :], w_out_ref.at[cut, :], out_sem.at[at])

        for at in range(steps):
            into(at).start()
        normed_ref[...] = layer_norm(resid_ref[...].astype(jnp.float32), gain_ref[...]).astype(jnp.bfloat16)
        for at in range(steps):
            into(at).wait()
            out_of(at).start()
            per = tile // step

            def one(i, carry, at=at):
                here = lanes(at * per + i, step)
                hidden, slope = gelu_and_slope(matmul(normed_ref[...], w_in_ref[:, here]))
                hid_ref[:, here] = hidden
                slope_ref[:, here] = slope
                return carry

            lax.fori_loop(0, per, one, 0)
        for at in range(steps):
            out_of(at).wait()

        def out_tile(i, carry):
            here = lanes(i, wide)
            out_ref[:, here] = matmul(hid_ref[...], w_out_ref[:, here]).astype(jnp.bfloat16)
            return carry

        lax.fori_loop(0, width // wide, out_tile, 0)

    shape = lambda *dims: jax.ShapeDtypeStruct(dims, jnp.bfloat16)
    return pl.pallas_call(
        kernel,
        in_specs=in_vmem(2) + [pl.BlockSpec(memory_space=pltpu.HBM)] * 2,
        out_specs=in_vmem(4),
        out_shape=[shape(rows, width), shape(rows, units), shape(rows, units), shape(rows, width)],
        scratch_shapes=[
            pltpu.VMEM((width, units), jnp.bfloat16),
            pltpu.VMEM((units, width), jnp.bfloat16),
            pltpu.SemaphoreType.DMA((steps,)),
            pltpu.SemaphoreType.DMA((steps,)),
        ],
        **params(4 * rows * width * units, 4 * width * units, 54),
    )(resid, gain, w_in, w_out)


def mlp_hidden(residuals, gain, w_in):
    rows, width = residuals[0].shape
    units = w_in.shape[1]
    step = next(c for c in (256, 128, units) if units % c == 0)
    count = len(residuals)

    def kernel(gain_ref, w_ref, *refs):
        normed_ref, hid_ref, slope_ref = refs[count:]
        for at, ref in enumerate(refs[:count]):
            here = slice(at * rows, (at + 1) * rows)
            normed_ref[here, :] = layer_norm(ref[...].astype(jnp.float32), gain_ref[...]).astype(jnp.bfloat16)
        per = units // step

        def one(at, carry):
            here, cut = lanes(at // per, rows), lanes(lax.rem(at, per), step)
            hidden, slope = gelu_and_slope(matmul(normed_ref[here, :], w_ref[:, cut]))
            hid_ref[here, cut] = hidden
            slope_ref[here, cut] = slope
            return carry

        lax.fori_loop(0, count * per, one, 0)

    shape = lambda cols: jax.ShapeDtypeStruct((count * rows, cols), jnp.bfloat16)
    return pl.pallas_call(
        kernel,
        in_specs=in_vmem(2 + count),
        out_specs=in_vmem(3),
        out_shape=[shape(width), shape(units), shape(units)],
        **params(2 * count * rows * width * units, 2 * width * units),
    )(gain, w_in, *residuals)


def chip_blocks(info, mine, theirs):
    n_chips, _, cols = mine[0].shape
    depths = [part.shape[1] for part in mine]
    count = len(mine)

    def kernel(info_ref, *refs):
        for back, out in enumerate(refs[2 * count :]):
            place = lax.rem(info_ref[1] + 2 * n_chips - 1 - back, n_chips)
            top = 0
            for own, other, depth in zip(refs[:count], refs[count : 2 * count], depths):
                value = own[place].astype(jnp.float32) + other[place].astype(jnp.float32)
                out[top : top + depth, :] = value.astype(jnp.bfloat16)
                top += depth

    return pl.pallas_call(
        kernel,
        in_specs=[pl.BlockSpec(memory_space=pltpu.SMEM)] + in_vmem(2 * count),
        out_specs=in_vmem(n_chips),
        out_shape=[jax.ShapeDtypeStruct((sum(depths), cols), jnp.bfloat16)] * n_chips,
        **params(n_chips * sum(depths) * cols, 6 * n_chips * sum(depths) * cols),
    )(info, *mine, *theirs)


def finish_sums(got, block, pieces):
    def kernel(got_ref, block_ref, *refs):
        for (row, depth, col, cols), ref in zip(pieces, refs):
            here = (slice(row, row + depth), slice(col, col + cols))
            ref[...] = got_ref[here].astype(jnp.float32) + block_ref[here].astype(jnp.float32)

    return pl.pallas_call(
        kernel,
        in_specs=in_vmem(2),
        out_specs=in_vmem(len(pieces)),
        out_shape=[jax.ShapeDtypeStruct((depth, cols), jnp.float32) for _, depth, _, cols in pieces],
        **params(got.size, 8 * got.size),
    )(got, block)


def mlp_back(info, halves, w_out, normed_cols, hiddens, slopes, n_chips):
    half, width = halves[0][0].shape
    count = len(halves)
    rows = 2 * half
    units = w_out.shape[0]
    chip_cols = width // n_chips
    share = chip_cols // 2
    flat = [part for pair in halves for part in pair]
    chunk = next(c for c in (512, 256, 128, units) if units % c == 0)
    chunks = units // chunk
    ahead = 2

    def kernel(info_ref, *refs):
        pieces = refs[: 2 * count]
        cols_ref, w_hbm, hid_a, hid_b, slope_a, slope_b, *refs = refs[2 * count :]
        own_in, own_out, their_in, their_out, *refs = refs
        w_ref, hid_ref, slope_ref, backs, back_hidden, back_cols, result, w_sem, slope_sem, hid_sem = refs
        core, chip, place = info_ref[0], info_ref[1], info_ref[2]
        first = hid_a.shape[0]
        spans = ((0, first), (first, count * rows))

        def copies(at):
            cut = pl.ds(at * chunk, chunk)
            parts = [pltpu.make_async_copy(w_hbm.at[cut, :], w_ref.at[cut, :], w_sem.at[at])]
            for which, (source, (top, end)) in enumerate(zip((slope_a, slope_b), spans)):
                here = slope_ref.at[pl.ds(top, end - top), cut]
                parts.append(pltpu.make_async_copy(source.at[:, cut], here, slope_sem.at[which, at]))
            return parts

        def hidden_copies():
            return [
                pltpu.make_async_copy(source, hid_ref.at[pl.ds(top, end - top), :], hid_sem.at[which])
                for which, (source, (top, end)) in enumerate(zip((hid_a, hid_b), spans))
            ]

        for at in range(min(ahead, chunks)):
            for copy in copies(at):
                copy.start()
        for at, ref in enumerate(pieces):
            which = place if at % 2 == 0 else 1 - place
            start = (at // 2) * rows + which * half
            backs[pl.ds(pl.multiple_of(start, half), half), :] = ref[...]
        for j in range(n_chips):

            @pl.when(chip == j)
            def _():
                back_cols[...] = backs[:, j * chip_cols : (j + 1) * chip_cols]

        for at in range(chunks):
            if at + ahead < chunks:
                for copy in copies(at + ahead):
                    copy.start()
            elif at + ahead == chunks or chunks < ahead and at == 0:
                for copy in hidden_copies():
                    copy.start()
            for copy in copies(at):
                copy.wait()
            for left, right in tiles(chunk):
                cut = slice(at * chunk + left, at * chunk + right)
                for image in range(count):
                    here = slice(image * rows, (image + 1) * rows)
                    grown = row_dot(backs[here, :], w_ref[cut, :])
                    back_hidden[here, cut] = (slope_ref[here, cut].astype(jnp.float32) * grown).astype(jnp.bfloat16)

        mine = pl.ds(pl.multiple_of(core * share, share), share)
        theirs = pl.ds(pl.multiple_of((1 - core) * share, share), share)

        def put(value, own, their, cut):
            result[...] = value
            own[:, cut] = result[mine, :]
            their[:, cut] = result[theirs, :].astype(jnp.bfloat16)

        spread = next(c for c in (640, 512, 256, 128, units) if units % c == 0)
        for lo, hi in tiles(units, spread):
            put(over_rows(cols_ref[...], back_hidden[:, lo:hi]), own_in, their_in, slice(lo, hi))
        for copy in hidden_copies():
            copy.wait()
        for lo, hi in tiles(units, spread):
            put(over_rows(back_cols[...], hid_ref[:, lo:hi]), own_out, their_out, slice(lo, hi))

    mine = jax.ShapeDtypeStruct((share, units), jnp.float32)
    theirs = jax.ShapeDtypeStruct((share, units), jnp.bfloat16)
    whole = lambda cols: pltpu.VMEM((count * rows, cols), jnp.bfloat16)
    spread = next(c for c in (640, 512, 256, 128, units) if units % c == 0)
    return pl.pallas_call(
        kernel,
        in_specs=[pl.BlockSpec(memory_space=pltpu.SMEM)]
        + in_vmem(2 * count + 1)
        + [pl.BlockSpec(memory_space=pltpu.HBM)] * 5,
        out_specs=in_vmem(4),
        out_shape=[mine, mine, theirs, theirs],
        scratch_shapes=[
            pltpu.VMEM((units, width), jnp.bfloat16),
            whole(units),
            whole(units),
            whole(width),
            whole(units),
            whole(chip_cols),
            pltpu.VMEM((chip_cols, spread), jnp.float32),
            pltpu.SemaphoreType.DMA((chunks,)),
            pltpu.SemaphoreType.DMA((2, chunks)),
            pltpu.SemaphoreType.DMA((2,)),
        ],
        **params(2 * count * rows * units * (width + 2 * chip_cols), 2 * units * (width + 3 * count * rows), 46),
    )(info, *flat, normed_cols, w_out, *hiddens, *slopes)


def route_features(info, owner, own, peer):
    images, patches, _ = own[0].shape
    n_chips = images // 2
    channels = 2 * sum(part.shape[2] for part in own)

    def kernel(info_ref, owner_ref, own_d, own_s, peer_d, peer_s, mine_ref, theirs_ref):
        core, chip, first = info_ref[0], info_ref[1], info_ref[2] == 0

        def one(image, carry):
            to = owner_ref[image]
            place = lax.rem(to // 2 - chip + n_chips, n_chips)
            pieces = []
            for here, there in ((own_d, peer_d), (own_s, peer_s)):
                a, b = here[image], there[image]
                pieces += [jnp.where(first, a, b), jnp.where(first, b, a)]
            joined = jnp.concatenate(pieces, axis=-1)

            @pl.when(lax.rem(to, 2) == core)
            def _():
                mine_ref[place] = joined

            @pl.when(lax.rem(to, 2) != core)
            def _():
                theirs_ref[place] = joined

            return carry

        lax.fori_loop(0, images, one, 0)

    return pl.pallas_call(
        kernel,
        in_specs=[pl.BlockSpec(memory_space=pltpu.SMEM)] * 2 + in_vmem(4),
        out_specs=in_vmem(2),
        out_shape=[jax.ShapeDtypeStruct((n_chips, patches, channels), jnp.bfloat16)] * 2,
        **params(images * patches * channels, 4 * images * patches * channels),
    )(info, owner, *own, *peer)


def pair_up(mine, theirs):
    n_chips, patches, channels = mine.shape

    def kernel(mine_ref, theirs_ref, *refs):
        for at, ref in enumerate(refs):
            ref[0] = mine_ref[at]
            ref[1] = theirs_ref[at]

    return pl.pallas_call(
        kernel,
        in_specs=in_vmem(2),
        out_specs=in_vmem(n_chips),
        out_shape=[jax.ShapeDtypeStruct((2, patches, channels), jnp.bfloat16)] * n_chips,
        **params(n_chips * patches * channels, 8 * n_chips * patches * channels),
    )(mine, theirs)


def adaptors_forward(resid, addends, gain, a_dino, a_sig, b_dino, b_sig):
    rows, width = resid.shape
    count = len(addends)
    wide, narrow = a_dino.shape[1], a_sig.shape[0]

    def kernel(resid_ref, gain_ref, ad_ref, as_ref, bd_ref, bs_ref, *refs):
        stream = resid_ref[...].astype(jnp.float32)
        added = refs[0][...].astype(jnp.float32)
        for ref in refs[1:count]:
            added = added + ref[...].astype(jnp.float32)
        stream = stream + added
        stream_ref, summary_ref, act_ref, slope_ref, pred_ref = refs[count:]
        stream_ref[...] = stream
        summary_ref[...] = layer_norm(stream, gain_ref[...]).astype(jnp.bfloat16)
        for lo, hi in tiles(narrow):
            act, slope = gelu_and_slope(row_dot(summary_ref[...], as_ref[lo:hi, :]))
            act_ref[:, wide + lo : wide + hi] = act
            slope_ref[:, wide + lo : wide + hi] = slope
        for lo, hi in tiles(bs_ref.shape[1]):
            value = matmul(act_ref[:, wide:], bs_ref[:, lo:hi])
            pred_ref[:, bd_ref.shape[1] + lo : bd_ref.shape[1] + hi] = value.astype(jnp.bfloat16)
        for lo, hi in tiles(wide):
            act, slope = gelu_and_slope(matmul(summary_ref[...], ad_ref[:, lo:hi]))
            act_ref[:, lo:hi] = act
            slope_ref[:, lo:hi] = slope
        for lo, hi in tiles(bd_ref.shape[1]):
            pred_ref[:, lo:hi] = matmul(act_ref[:, :wide], bd_ref[:, lo:hi]).astype(jnp.bfloat16)

    shape = lambda cols, dtype=jnp.bfloat16: jax.ShapeDtypeStruct((rows, cols), dtype)
    work = width * (wide + narrow) + b_dino.size + b_sig.size
    return pl.pallas_call(
        kernel,
        in_specs=in_vmem(6 + count),
        out_specs=in_vmem(5),
        out_shape=[
            shape(width, jnp.float32),
            shape(width),
            shape(wide + narrow),
            shape(wide + narrow),
            shape(b_dino.shape[1] + b_sig.shape[1]),
        ],
        **params(2 * rows * work, 2 * work),
    )(resid, gain, a_dino, a_sig, b_dino, b_sig, *addends)


def loss_rows(info_ref, addends, targets, start, back_ref, factor):
    rows, channels = back_ref.shape
    core, chip = info_ref[0], info_ref[1]
    n_from, patches = len(targets), targets[0].shape[-2]

    def block(here, goal):
        goal = goal.astype(jnp.float32)
        value = addends[0][here, start : start + channels].astype(jnp.float32)
        for ref in addends[1:]:
            value = value + ref[here, start : start + channels].astype(jnp.float32)
        norm_pred = jnp.sum(value * value, axis=-1, keepdims=True) + channels * EPS
        norm_target = jnp.sum(goal * goal, axis=-1, keepdims=True) + channels * EPS
        recip = lax.rsqrt(norm_pred * norm_target)
        cosine = jnp.sum(value * goal, axis=-1, keepdims=True) * recip
        of_pred = factor * (1.0 + channels * (cosine / norm_pred))
        of_target = factor * (1.0 + channels * recip)
        back_ref[here, :] = (value * of_pred - goal * of_target).astype(jnp.bfloat16)

    for at, ref in enumerate(targets):
        if len(ref.shape) == 2:
            for lo, hi in tiles(rows, 32):
                block(slice(lo, hi), ref[lo:hi, start : start + channels])
            continue
        source = lax.rem(chip - at + n_from, n_from)
        for other in range(2):
            place = 2 * source + (1 - core if other else core)
            here = pl.ds(pl.multiple_of(place * patches, patches), patches)
            block(here, ref[other, :, start : start + channels])


def adaptors_back(info, addends, targets, b_weights, slope, a_weights, factor):
    rows = addends[0].shape[0]
    width = a_weights[0].shape[0]
    units = [w.shape[0] for w in b_weights]
    count = len(addends) + len(targets)

    def kernel(info_ref, *refs):
        b_d, b_s, slope_ref, a_d, a_s, back_d, back_s, down_ref, part_ref = refs[count:]
        for start, back in ((0, back_d), (b_d.shape[1], back_s)):
            loss_rows(info_ref, refs[: len(addends)], refs[len(addends) : count], start, back, factor)
        start = 0
        for back, weights in ((back_d, b_d), (back_s, b_s)):
            for lo, hi in tiles(weights.shape[0]):
                grown = row_dot(back[...], weights[lo:hi, :])
                down = slope_ref[:, start + lo : start + hi].astype(jnp.float32) * grown
                down_ref[:, start + lo : start + hi] = down.astype(jnp.bfloat16)
            start += weights.shape[0]
        for lo, hi in tiles(width):
            total = row_dot(down_ref[:, : units[0]], a_d[lo:hi, :])
            total = total + matmul(down_ref[:, units[0] :], a_s[:, lo:hi])
            part_ref[:, lo:hi] = total.astype(jnp.bfloat16)

    work = sum(u * (w.shape[1] + width) for u, w in zip(units, b_weights))
    shape = lambda cols: jax.ShapeDtypeStruct((rows, cols), jnp.bfloat16)
    return pl.pallas_call(
        kernel,
        in_specs=[pl.BlockSpec(memory_space=pltpu.SMEM)] + in_vmem(count + 5),
        out_specs=in_vmem(4),
        out_shape=[*(shape(w.shape[1]) for w in b_weights), shape(sum(units)), shape(width)],
        **params(2 * rows * work, 2 * work, 48),
    )(info, *addends, *targets, *b_weights, slope, *a_weights)


def gradient_blocks(core, pairs, n_blocks):
    rows = pairs[0][0].shape[0]
    depths = [left.shape[1] // n_blocks for left, _, _ in pairs]
    depth = max(depths)
    widths = [cols.stop - cols.start for _, _, cols in pairs]
    count = len(pairs)

    def kernel(core_ref, *refs):
        own = core_ref[0]
        mine_ref, theirs_ref = refs[2 * count :]

        def put(value, at, per, start):
            row = at
            while row < at + value.shape[0]:
                block, inside = row // per, row % per
                stop = min(at + value.shape[0], (block + 1) * per)
                piece = value[row - at : stop - at]
                place = (block // 2, slice(inside, inside + stop - row), slice(start, start + value.shape[1]))

                @pl.when(own == block % 2)
                def _():
                    mine_ref[place] = piece

                @pl.when(own != block % 2)
                def _():
                    theirs_ref[place] = piece

                row = stop

        start = 0
        for at, (per, width) in enumerate(zip(depths, widths)):
            left, right, cols = refs[2 * at], refs[2 * at + 1], pairs[at][2]
            if per < depth:
                blank = jnp.zeros((n_blocks // 2, depth - per, width), jnp.bfloat16)
                mine_ref[:, per:, start : start + width] = blank
                theirs_ref[:, per:, start : start + width] = blank
            for lo, hi in tiles(left.shape[1]):
                value = lax.dot_general(
                    left[:, lo:hi], right[:, cols], (((0,), (0,)), ((), ())), preferred_element_type=jnp.float32
                )
                put(value.astype(jnp.bfloat16), lo, per, start)
            start += width

    work = rows * sum(left.shape[1] * width for (left, _, _), width in zip(pairs, widths))
    return pl.pallas_call(
        kernel,
        in_specs=[pl.BlockSpec(memory_space=pltpu.SMEM)] + in_vmem(2 * count),
        out_specs=in_vmem(2),
        out_shape=[jax.ShapeDtypeStruct((n_blocks // 2, depth, sum(widths)), jnp.bfloat16)] * 2,
        **params(2 * work, 2 * n_blocks * depth * sum(widths)),
    )(core.astype(jnp.int32).reshape(1), *[array for pair in pairs for array in pair[:2]])


def matmul(left, right):
    return jnp.dot(left, right, preferred_element_type=jnp.float32)


def contract_rows(left, right):
    return lax.dot_general(
        left, right, (((0,), (0,)), ((), ())), preferred_element_type=jnp.float32
    )


def contract_cols(left, right):
    return lax.dot_general(
        left, right, (((1,), (1,)), ((), ())), preferred_element_type=jnp.float32
    )


def shift(values, axis, by=1):
    count = lax.axis_size(axis)
    return lax.ppermute(values, axis, [(i, (i + by) % count) for i in range(count)])


def addends_mp(part):
    if lax.axis_size("mp") == 2:
        return (part, shift(part, "mp"))
    return (lax.psum(part, "mp"),)


def in_order(own, other, axis):
    first = lax.axis_index("mp") == 0
    return jnp.concatenate(
        [jnp.where(first, own, other), jnp.where(first, other, own)], axis=axis
    )


def tie(*values):
    return lax.optimization_barrier(values)


def back_rows(place, stream, part, other, gain):
    half, width = other.shape

    def kernel(place_ref, stream_ref, part_ref, other_ref, gain_ref, back_ref):
        here = pl.ds(pl.multiple_of(place_ref[0] * half, half), half)
        upstream = part_ref[here, :].astype(jnp.float32) + other_ref[...].astype(jnp.float32)
        back_ref[...] = norm_back(stream_ref[here, :], gain_ref[...], upstream).astype(jnp.bfloat16)

    return pl.pallas_call(
        kernel,
        in_specs=[pl.BlockSpec(memory_space=pltpu.SMEM)] + in_vmem(4),
        out_specs=pl.BlockSpec(memory_space=pltpu.VMEM),
        out_shape=jax.ShapeDtypeStruct((half, width), jnp.bfloat16),
        **params(20 * half * width, 12 * half * width),
    )(place, stream, part, other, gain)


def per_device(
    resid,
    gain_mlp,
    gain_out,
    w_in,
    w_out,
    a_dino,
    b_dino,
    a_sig,
    b_sig,
    dino_feats,
    sig_feats,
    owner,
):
    n_chips = lax.axis_size("dp")
    n_cores = lax.axis_size("teach")
    width = resid.shape[2]
    rows = resid.shape[0] * resid.shape[1]
    factor = 1.0 / math.sqrt(n_chips * n_cores * rows)
    total_images = owner.shape[0]
    chip = lax.axis_index("dp")
    core = lax.axis_index("teach")

    two = lax.axis_size("mp") == 2
    resid = resid.reshape(rows, width)
    info = jnp.stack([core, chip, lax.axis_index("mp")]).astype(jnp.int32)
    feats = (dino_feats, sig_feats)
    ring_r = [shift(resid, "dp", -1)]
    if two:
        peers = [shift(part, "mp") for part in feats]
    normed, hidden, slope, out_part = mlp_forward(resid, gain_mlp, w_in, w_out)
    if two:
        *peers, ring_r[0], out_part = tie(*peers, ring_r[0], out_part)
    out_addends = addends_mp(out_part)
    if n_chips > 2:
        ring_r.append(shift(ring_r[0], "dp", -1))
    if two:
        mine, theirs = route_features(info, owner, feats, peers)
        blocks = pair_up(mine, shift(theirs, "teach"))
        *blocks, ring_r[-1], arrived = tie(*blocks, ring_r[-1], out_addends[1])
        out_addends = (out_part, arrived)
        targets = [blocks[0]] + [shift(blocks[k], "dp", k) for k in range(1, n_chips)]
    else:
        images = jnp.arange(total_images, dtype=jnp.int32)
        inverse = jnp.sum(jnp.where(owner[None, :] == images[:, None], images[None, :], 0), axis=1)
        feats = [lax.all_gather(part, "mp", axis=2, tiled=True) for part in feats]
        sent = jnp.concatenate(feats, axis=2)
        sent = sent.at[inverse].get(mode="promise_in_bounds", unique_indices=True)
        got = lax.all_to_all(sent, ("dp", "teach"), split_axis=0, concat_axis=1, tiled=True)
        targets = [got.reshape(rows, -1)]

    a_sig_t = a_sig.T
    n_units = b_dino.shape[0]
    stream, summary, act, slope_t, pred = adaptors_forward(
        resid, out_addends, gain_out, a_dino, a_sig_t, b_dino, b_sig
    )
    pred_addends = addends_mp(pred)
    while len(ring_r) < n_chips - 1:
        ring_r[-1], *_ = tie(ring_r[-1], *pred_addends)
        ring_r.append(shift(ring_r[-1], "dp", -1))
    back_dino, back_sig, down, part = adaptors_back(
        info, pred_addends, targets, (b_dino, b_sig), slope_t, (a_dino, a_sig_t), factor
    )

    n_blocks = n_chips * n_cores
    cols_d, cols_s = slice(0, n_units), slice(n_units, n_units + b_sig.shape[0])
    mine_b, theirs_b = gradient_blocks(core, [(back_dino, act, cols_d), (back_sig, act, cols_s)], n_blocks)
    mine_a, theirs_a = gradient_blocks(core, [(summary, down, slice(0, down.shape[1]))], n_blocks)
    if two:
        half = rows // 2
        place = lax.axis_index("mp").astype(jnp.int32).reshape(1)
        other = shift(lax.dynamic_slice_in_dim(part, (1 - place[0]) * half, half, 0), "mp")
        other, theirs_b, theirs_a, ring_r[-1] = tie(other, theirs_b, theirs_a, ring_r[-1])
        back = back_rows(place, stream, part, other, gain_out)
    else:
        back = norm_back(stream, gain_out, addends_mp(part)[0].astype(jnp.float32)).astype(jnp.bfloat16)

    held_s = [back]
    rows_in, got_b, got_a = tie(shift(back, "dp", -1), shift(theirs_b, "teach"), shift(theirs_a, "teach"))
    if two:
        swapped = [shift(back, "mp")]
        swapped[0], rows_in = tie(swapped[0], rows_in)
    held_s.append(rows_in)
    held, *sums = chip_blocks(info, (mine_a, mine_b), (got_a, got_b))

    def columns(values, at, count):
        return lax.dynamic_slice_in_dim(values, at * count, count, 1)

    others = tie(*ring_r, held_s[1])[:-1]
    others, other_hidden, other_slope = mlp_hidden(others, gain_mlp, w_in)
    normeds = jnp.concatenate([normed, others], axis=0)
    normed_cols = columns(normeds, chip, width // n_chips)
    sums_in = shift(held, "dp")
    for step in range(2, n_chips):
        rows_in = shift(held_s[-1], "dp", -1)
        if step == 2:
            rows_in, other_slope = tie(rows_in, other_slope)
        if two:
            last, rows_in = tie(shift(held_s[-1], "mp"), rows_in)
            swapped.append(last)
        if step == n_chips - 1:
            rows_in, sums_in = tie(rows_in, sums_in)
        held_s.append(rows_in)
    hiddens, slopes = (hidden, other_hidden), (slope, other_slope)
    for step in range(1, n_chips - 1):
        held = (sums_in.astype(jnp.float32) + sums[step - 1].astype(jnp.float32)).astype(jnp.bfloat16)
        sums_in = shift(held, "dp")
        if two and step == max(1, n_chips - 3):
            swapped += [shift(part, "mp") for part in held_s[len(swapped) :]]
            halves = list(zip(held_s, swapped))
            outs = mlp_back(info, halves, w_out, normed_cols, hiddens, slopes, n_chips)
            sums_in, own_in, own_out, their_in, their_out = tie(sums_in, *outs)
    if two:
        adds = [(own_in, shift(their_in, "teach")), (own_out, shift(their_out, "teach"))]
    else:
        backs = jnp.concatenate(held_s, axis=0)
        back_hidden = (jnp.concatenate(slopes, axis=0) * contract_cols(backs, w_out)).astype(jnp.bfloat16)
        share = width // n_blocks
        place = chip * n_cores + core
        peer = chip * n_cores + (1 - core)
        all_hidden = jnp.concatenate(hiddens, axis=0)
        sent_out = contract_rows(all_hidden, columns(backs, peer, share)).astype(jnp.bfloat16)
        sent_in = contract_rows(columns(normeds, peer, share), back_hidden).astype(jnp.bfloat16)
        own_out = contract_rows(all_hidden, columns(backs, place, share)).T
        own_in = contract_rows(columns(normeds, place, share), back_hidden)
        adds = [(own_in, shift(sent_in, "teach")), (own_out, shift(sent_out.T, "teach"))]
    depth_a = mine_a.shape[1]
    depth_d, depth_s = (b.shape[1] // n_blocks for b in (b_dino, b_sig))
    narrow = b_sig.shape[0]
    out_wi, out_wo = [own + got.astype(jnp.float32) for own, got in adds]
    sums_in, out_wi, out_wo = tie(sums_in, out_wi, out_wo)
    out_a_d, out_a_s, out_b_d, out_b_s = finish_sums(
        sums_in,
        sums[-1],
        [(0, depth_a, 0, n_units), (0, depth_a, n_units, narrow), (depth_a, depth_d, 0, n_units), (depth_a, depth_s, n_units, narrow)],
    )
    out_wo, out_b_d, out_b_s = out_wo.T, out_b_d.T, out_b_s.T
    return out_wi, out_wo, out_a_d, out_b_d, out_a_s, out_b_s


def solution(mesh):
    placed = (
        P(("groups", "dp", "teach"), None, None),
        P(),
        P(),
        P(None, "mp"),
        P("mp", None),
        P(None, "mp"),
        P("mp", None),
        P(None, "mp"),
        P("mp", None),
        P("groups", ("dp", "teach"), "mp"),
        P("groups", ("dp", "teach"), "mp"),
        P("groups"),
    )
    return jax.shard_map(
        per_device,
        mesh=mesh,
        in_specs=placed,
        out_specs=(
            P(("groups", "dp", "teach"), "mp"),
            P(("groups", "mp"), ("dp", "teach")),
            P(("groups", "dp", "teach"), "mp"),
            P(("groups", "mp"), ("dp", "teach")),
            P(("groups", "dp", "teach"), "mp"),
            P(("groups", "mp"), ("dp", "teach")),
        ),
        check_vma=False,
    )
```

profile of v0, /device:TPU:0, one launch (start us, length us, event | category | flops | bytes accessed | tf_op | source)
XLA Modules:
  0.0 212.3 jit_solution(4223315209012321605)
XLA Ops:
  0.6 5.1 %collective-permute-start.2 = (bf16[256,1280]{1,0:T(8,128)(2,1)}, bf16[256,1280]{1,0:T(8,128)(2,1)S(1)}, u32[]{:S(2)}, u32[]{:S(2)}) collective-permute-start(bf16[256,1280]{1,0:T(8,128)(2,1)} %bitcast.12), channel_id=1, source_target_pairs={{0,12},{4,0},{8,4},{12,8},{1,13},{5,1},{9,5},{13,9},{2,14},{6,2},{... | collective-permute-start | bytes 1966088 | tf_op jit(solution)/shard_map/ppermute | solution.py:542
  5.7 1.5 collective-permute-start.1
  7.2 0.5 collective-permute-start
  7.8 0.1 pad_add_fusion.info_ref
  7.9 12.4 %shard_map.163 = (bf16[256,1280]{1,0:T(8,128)(2,1)}, bf16[256,2560]{1,0:T(8,128)(2,1)}, bf16[256,2560]{1,0:T(8,128)(2,1)}, bf16[256,1280]{1,0:T(8,128)(2,1)}) custom-call(bf16[256,1280]{1,0:T(8,128)(2,1)} %bitcast.13, f32[1280]{0:T(1024)} %gain_ref.7, bf16[1280,2560]{1,0:T(8,128)(2,1)} %w_ref.1, bf16[2560,1280]{1,0:T(8,128)(2,1)} %refs_9_.3), custom_call_target="tpu_custom_call" | custom-call | flops 3355443200 | bytes 13107200 | tf_op jit(solution)/shard_map/pallas_call | solution.py:116
  20.3 3.2 %collective-permute-done.peer_d = bf16[8,32,768]{2,1,0:T(8,128)(2,1)S(1)} collective-permute-done((bf16[8,32,768]{2,1,0:T(8,128)(2,1)}, bf16[8,32,768]{2,1,0:T(8,128)(2,1)S(1)}, u32[]{:S(2)}, u32[]{:S(2)}) %collective-permute-start) | collective-permute-done | bytes 393248 | tf_op jit(solution)/shard_map/ppermute | solution.py:542
  23.6 1.3 shard_map.164
  24.9 0.1 collective-permute-start.3
  25.0 1.6 collective-permute-start.5
  26.5 0.7 collective-permute-start.4
  27.2 0.9 shard_map.165
  28.1 14.2 %collective-permute-done.5.refs_1_ = bf16[256,1280]{1,0:T(8,128)(2,1)S(1)} collective-permute-done((bf16[256,1280]{1,0:T(8,128)(2,1)}, bf16[256,1280]{1,0:T(8,128)(2,1)S(1)}, u32[]{:S(2)}, u32[]{:S(2)}) %collective-permute-start.5) | collective-permute-done | bytes 655392 | tf_op jit(solution)/shard_map/ppermute | solution.py:542
  42.3 1.1 collective-permute-done.4.refs_1_
  43.5 1.1 copy-done.11
  44.6 4.7 %shard_map.166 = (f32[256,1280]{1,0:T(8,128)S(1)}, bf16[256,1280]{1,0:T(8,128)(2,1)S(1)}, bf16[256,1344]{1,0:T(8,128)(2,1)S(1)}, bf16[256,1344]{1,0:T(8,128)(2,1)S(1)}, bf16[256,2688]{1,0:T(8,128)(2,1)}) custom-call(bf16[256,1280]{1,0:T(8,128)(2,1)S(1)} %bitcast.14, f32[1280]{0:T(1024)S(1)} %copy-done.14, bf16[1280,768]{1,0:T(8,128)(2,1)S(1)} %copy-done.1, ...), custom_call_target="tpu_custom_call" | custom-call | flops 1824522240 | bytes 7127040 | tf_op jit(solution)/shard_map/pallas_call | solution.py:393
  49.3 1.1 copy-done.6
  50.3 0.8 copy-done.19
  51.2 0.8 copy-done.23
  52.0 0.5 collective-permute-start.6
  52.6 3.0 %collective-permute-start.8 = (bf16[2,32,2688]{2,1,0:T(8,128)(2,1)}, bf16[2,32,2688]{2,1,0:T(8,128)(2,1)S(1)}, u32[]{:S(2)}, u32[]{:S(2)}) collective-permute-start(bf16[2,32,2688]{2,1,0:T(8,128)(2,1)} %get-tuple-element.99), channel_id=1, source_target_pairs={{0,8},{4,12},{8,0},{12,4},{1,9},{5,13},{9,1},{13,5},{2,10},{6,14},... | collective-permute-start | bytes 1032200 | tf_op jit(solution)/shard_map/ppermute | solution.py:542
  55.6 0.8 collective-permute-start.9
  56.4 27.4 %collective-permute-done.6.refs_1_ = bf16[256,2688]{1,0:T(8,128)(2,1)} collective-permute-done((bf16[256,2688]{1,0:T(8,128)(2,1)}, bf16[256,2688]{1,0:T(8,128)(2,1)}, u32[]{:S(2)}, u32[]{:S(2)}) %collective-permute-start.6) | collective-permute-done | bytes 1376288 | tf_op jit(solution)/shard_map/ppermute | solution.py:542
  83.8 2.5 %collective-permute-start.11 = (bf16[256,1280]{1,0:T(8,128)(2,1)}, bf16[256,1280]{1,0:T(8,128)(2,1)S(1)}, u32[]{:S(2)}, u32[]{:S(2)}) collective-permute-start(bf16[256,1280]{1,0:T(8,128)(2,1)} %collective-permute-done.4.refs_1_), channel_id=1, source_target_pairs={{0,12},{4,0},{8,4},{12,8},{1,13},{5,1},{9,5},{13,9},{2,14},{6,2},{... | collective-permute-start | bytes 1966088 | tf_op jit(solution)/shard_map/ppermute | solution.py:542
  86.3 1.3 copy-done.4
  87.6 7.4 %shard_map.167 = (bf16[256,1536]{1,0:T(8,128)(2,1)S(1)}, bf16[256,1152]{1,0:T(8,128)(2,1)S(1)}, bf16[256,1344]{1,0:T(8,128)(2,1)S(1)}, bf16[256,1280]{1,0:T(8,128)(2,1)S(1)}) custom-call(s32[3]{0:T(128)S(1)} %pad_add_fusion.info_ref, bf16[256,2688]{1,0:T(8,128)(2,1)} %get-tuple-element.96.refs_0_, bf16[256,2688]{1,0:T(8,128)(2,1)} %collective-permute-done.6.refs_1_, ...), custom_call_target="tpu_custom_call" | custom-call | flops 1824522240 | bytes 7127040 | tf_op jit(solution)/shard_map/pallas_call | solution.py:462
  95.0 0.6 collective-permute-start.10
  95.7 2.3 %shard_map.169 = (bf16[4,160,1344]{2,1,0:T(8,128)(2,1)S(1)}, bf16[4,160,1344]{2,1,0:T(8,128)(2,1)S(1)}) custom-call(s32[1]{0:T(128)} %bitcast.3.core_ref, bf16[256,1280]{1,0:T(8,128)(2,1)S(1)} %copy-done.24, bf16[256,1344]{1,0:T(8,128)(2,1)S(1)} %get-tuple-element.108.refs_1_), custom_call_target="tpu_custom_call" | custom-call | flops 880803840 | bytes 3440640 | tf_op jit(solution)/shard_map/pallas_call | solution.py:515
  98.0 4.0 %shard_map.168 = (bf16[4,192,1344]{2,1,0:T(8,128)(2,1)S(1)}, bf16[4,192,1344]{2,1,0:T(8,128)(2,1)S(1)}) custom-call(s32[1]{0:T(128)} %bitcast.3.core_ref, bf16[256,1536]{1,0:T(8,128)(2,1)S(1)} %get-tuple-element.103.refs_0_, bf16[256,1344]{1,0:T(8,128)(2,1)S(1)} %copy-done.20, bf16[256,1152]{1,0:T(8,128)(2,1)S(1)} %get-tuple-element.105.refs_2_, ...), custom_call_target="tpu_custom_call" | custom-call | flops 943718400 | bytes 4128768 | tf_op jit(solution)/shard_map/pallas_call | solution.py:515
  102.0 0.8 collective-permute-done.10.other_ref
  102.9 0.5 collective-permute-start.15
  103.4 0.5 shard_map.170.refs_0_
  103.8 0.5 collective-permute-start.13
  104.3 0.5 collective-permute-start.12
  104.9 8.6 %collective-permute-done.13.refs_2_ = bf16[128,1280]{1,0:T(8,128)(2,1)S(1)} collective-permute-done((bf16[128,1280]{1,0:T(8,128)(2,1)S(1)}, bf16[128,1280]{1,0:T(8,128)(2,1)S(1)}, u32[]{:S(2)}, u32[]{:S(2)}) %collective-permute-start.13) | collective-permute-done | bytes 327712 | tf_op jit(solution)/shard_map/ppermute | solution.py:542
  113.6 2.2 %shard_map.172 = (bf16[352,1344]{1,0:T(8,128)(2,1)}, bf16[352,1344]{1,0:T(8,128)(2,1)S(1)}, bf16[352,1344]{1,0:T(8,128)(2,1)S(1)}, bf16[352,1344]{1,0:T(8,128)(2,1)S(1)}) custom-call(s32[3]{0:T(128)S(1)} %pad_add_fusion.info_ref, bf16[4,160,1344]{2,1,0:T(8,128)(2,1)S(1)} %get-tuple-element.125.refs_0_, bf16[4,192,1344]{2,1,0:T(8,128)(2,1)S(1)} %get-tuple-element.126.refs_1_, ...), custom_call_target="tpu_custom_call" | custom-call | flops 1892352 | bytes 11354112 | tf_op jit(solution)/shard_map/pallas_call | solution.py:177
  115.7 1.0 copy-done.8
  116.7 0.5 collective-permute-start.20
  117.2 0.7 copy-done.27
  118.0 3.3 %collective-permute-start.17 = (bf16[128,1280]{1,0:T(8,128)(2,1)S(1)}, bf16[128,1280]{1,0:T(8,128)(2,1)}, u32[]{:S(2)}, u32[]{:S(2)}) collective-permute-start(bf16[128,1280]{1,0:T(8,128)(2,1)S(1)} %collective-permute-done.13.refs_2_), channel_id=1, source_target_pairs={{0,12},{4,0},{8,4},{12,8},{1,13},{5,1},{9,5},{13,9},{2,14},{6,2},{... | collective-permute-start | bytes 983048 | tf_op jit(solution)/shard_map/ppermute | solution.py:542
  121.3 0.8 collective-permute-start.16
  122.1 16.2 %shard_map.171 = (bf16[768,1280]{1,0:T(8,128)(2,1)S(1)}, bf16[768,2560]{1,0:T(8,128)(2,1)S(1)}, bf16[768,2560]{1,0:T(8,128)(2,1)S(1)}) custom-call(f32[1280]{0:T(1024)S(1)} %copy-done.15, bf16[1280,2560]{1,0:T(8,128)(2,1)S(1)} %bitcast.9, bf16[256,1280]{1,0:T(8,128)(2,1)S(1)} %copy-done.22, bf16[256,1280]{1,0:T(8,128)(2,1)} %collective-permute-done.4.refs_1_, ...), custom_call_target="tpu_custom_call" | custom-call | flops 5033164800 | bytes 6553600 | tf_op jit(solution)/shard_map/pallas_call | solution.py:154
  138.3 1.9 copy-done.31
  140.2 1.9 copy-done.32
  142.2 5.7 %collective-permute-done.17.refs_4_ = bf16[128,1280]{1,0:T(8,128)(2,1)} collective-permute-done((bf16[128,1280]{1,0:T(8,128)(2,1)S(1)}, bf16[128,1280]{1,0:T(8,128)(2,1)}, u32[]{:S(2)}, u32[]{:S(2)}) %collective-permute-start.17) | collective-permute-done | bytes 327712 | tf_op jit(solution)/shard_map/ppermute | solution.py:542
  147.9 0.7 copy-done.29
  148.6 1.5 collective-permute-start.19
  150.2 1.2 collective-permute-start.18
  151.3 6.2 %collective-permute-done.19.refs_6_ = bf16[128,1280]{1,0:T(8,128)(2,1)} collective-permute-done((bf16[128,1280]{1,0:T(8,128)(2,1)}, bf16[128,1280]{1,0:T(8,128)(2,1)}, u32[]{:S(2)}, u32[]{:S(2)}) %collective-permute-start.19) | collective-permute-done | bytes 327712 | tf_op jit(solution)/shard_map/ppermute | solution.py:542
  157.6 0.6 collective-permute-done.18.refs_5_
  158.1 1.1 collective-permute-start.22
  159.2 1.8 add_convert_fusion.1
  161.0 1.5 collective-permute-start.21
  162.5 0.5 fusion.refs_8_
  163.0 2.4 %collective-permute-done.22.refs_7_ = bf16[128,1280]{1,0:T(8,128)(2,1)S(1)} collective-permute-done((bf16[128,1280]{1,0:T(8,128)(2,1)}, bf16[128,1280]{1,0:T(8,128)(2,1)S(1)}, u32[]{:S(2)}, u32[]{:S(2)}) %collective-permute-start.22) | collective-permute-done | bytes 327712 | tf_op jit(solution)/shard_map/ppermute | solution.py:542
  165.5 16.6 %shard_map.173 = (f32[160,2560]{1,0:T(8,128)}, f32[160,2560]{1,0:T(8,128)}, bf16[160,2560]{1,0:T(8,128)(2,1)S(1)}, bf16[160,2560]{1,0:T(8,128)(2,1)S(1)}) custom-call(s32[3]{0:T(128)S(1)} %pad_add_fusion.info_ref, bf16[128,1280]{1,0:T(8,128)(2,1)S(1)} %shard_map.170.refs_0_, bf16[128,1280]{1,0:T(8,128)(2,1)S(1)} %copy-done.28, ...), custom_call_target="tpu_custom_call" | custom-call | flops 10066329600 | bytes 22282240 | tf_op jit(solution)/shard_map/pallas_call | solution.py:285
  182.1 2.3 %collective-permute-done.21 = bf16[352,1344]{1,0:T(8,128)(2,1)S(1)} collective-permute-done((bf16[352,1344]{1,0:T(8,128)(2,1)S(1)}, bf16[352,1344]{1,0:T(8,128)(2,1)S(1)}, u32[]{:S(2)}, u32[]{:S(2)}) %collective-permute-start.21) | collective-permute-done | bytes 946208 | tf_op jit(solution)/shard_map/ppermute | solution.py:542
  184.4 0.5 collective-permute-start.25
  184.9 0.3 add_convert_fusion
  185.2 0.1 collective-permute-start.23
  185.3 1.5 collective-permute-done.24
  186.8 1.3 convert_add_fusion.1
  188.1 1.3 convert_add_fusion
  189.4 21.5 %collective-permute-done.23.got_ref = bf16[352,1344]{1,0:T(8,128)(2,1)S(1)} collective-permute-done((bf16[352,1344]{1,0:T(8,128)(2,1)S(1)}, bf16[352,1344]{1,0:T(8,128)(2,1)S(1)}, u32[]{:S(2)}, u32[]{:S(2)}) %collective-permute-start.23) | collective-permute-done | bytes 946208 | tf_op jit(solution)/shard_map/ppermute | solution.py:542
  210.9 1.4 shard_map.174
  (84 shorter events, 0.2 us)
Async XLA Ops:
  0.6 22.9 %collective-permute-start.2 = (bf16[256,1280]{1,0:T(8,128)(2,1)}, bf16[256,1280]{1,0:T(8,128)(2,1)S(1)}, u32[]{:S(2)}, u32[]{:S(2)}) collective-permute-start(bf16[256,1280]{1,0:T(8,128)(2,1)} %bitcast.12), channel_id=1, source_target_pairs={{0,12},{4,0},{8,4},{12,8},{1,13},{5,1},{9,5},{13,9},{2,14},{6,2},{... | collective-permute-start | bytes 1966088 | tf_op jit(solution)/shard_map/ppermute | solution.py:542
  5.7 14.6 %collective-permute-start.1 = (bf16[8,32,576]{2,1,0:T(8,128)(2,1)}, bf16[8,32,576]{2,1,0:T(8,128)(2,1)S(1)}, u32[]{:S(2)}, u32[]{:S(2)}) collective-permute-start(bf16[8,32,576]{2,1,0:T(8,128)(2,1)} %own_s.1), channel_id=1, source_target_pairs={{0,2},{2,0},{1,3},{3,1},{4,6},{6,4},{5,7},{7,5},{8,10},{10,8},{9,1... | collective-permute-start | bytes 884744 | tf_op jit(solution)/shard_map/ppermute | solution.py:542
  7.2 16.3 %collective-permute-start = (bf16[8,32,768]{2,1,0:T(8,128)(2,1)}, bf16[8,32,768]{2,1,0:T(8,128)(2,1)S(1)}, u32[]{:S(2)}, u32[]{:S(2)}) collective-permute-start(bf16[8,32,768]{2,1,0:T(8,128)(2,1)} %own_d.1), channel_id=1, source_target_pairs={{0,2},{2,0},{1,3},{3,1},{4,6},{6,4},{5,7},{7,5},{8,10},{10,8},{9,1... | collective-permute-start | bytes 1179656 | tf_op jit(solution)/shard_map/ppermute | solution.py:542
  7.8 15.7 %copy-start.12 = (bf16[8,32,768]{2,1,0:T(8,128)(2,1)S(1)}, bf16[8,32,768]{2,1,0:T(8,128)(2,1)}, u32[]{:S(2)}) copy-start(bf16[8,32,768]{2,1,0:T(8,128)(2,1)} %own_d.1) | copy-start | bytes 1179652
  7.8 15.7 %copy-start.13 = (bf16[8,32,576]{2,1,0:T(8,128)(2,1)S(1)}, bf16[8,32,576]{2,1,0:T(8,128)(2,1)}, u32[]{:S(2)}) copy-start(bf16[8,32,576]{2,1,0:T(8,128)(2,1)} %own_s.1) | copy-start | bytes 884740
  7.8 15.7 %copy-start.16 = (s32[8]{0:T(128)S(1)}, s32[8]{0:T(128)}, u32[]{:S(2)}) copy-start(s32[8]{0:T(128)} %owner_ref.1) | copy-start | bytes 100
  7.8 35.6 %copy-start.1 = (bf16[1280,768]{1,0:T(8,128)(2,1)S(1)}, bf16[1280,768]{1,0:T(8,128)(2,1)}, u32[]{:S(2)}) copy-start(bf16[1280,768]{1,0:T(8,128)(2,1)} %refs_9_.2) | copy-start | bytes 5898244
  7.8 35.6 %copy-start.2 = (bf16[1280,576]{0,1:T(8,128)(2,1)S(1)}, bf16[1280,576]{0,1:T(8,128)(2,1)}, u32[]{:S(2)}) copy-start(bf16[1280,576]{0,1:T(8,128)(2,1)} %param.19) | copy-start | bytes 4423684
  7.9 35.6 %copy-start.3 = (bf16[576,1152]{1,0:T(8,128)(2,1)S(1)}, bf16[576,1152]{1,0:T(8,128)(2,1)}, u32[]{:S(2)}) copy-start(bf16[576,1152]{1,0:T(8,128)(2,1)} %refs_7_.1) | copy-start | bytes 3981316
  7.9 35.6 %copy-start.5 = (bf16[1,256,1280]{2,1,0:T(8,128)(2,1)S(1)}, bf16[1,256,1280]{2,1,0:T(8,128)(2,1)}, u32[]{:S(2)}) copy-start(bf16[1,256,1280]{2,1,0:T(8,128)(2,1)} %param.12) | copy-start | bytes 1966084
  20.3 23.1 %copy-start = (bf16[768,1536]{1,0:T(8,128)(2,1)S(1)}, bf16[768,1536]{1,0:T(8,128)(2,1)}, u32[]{:S(2)}) copy-start(bf16[768,1536]{1,0:T(8,128)(2,1)} %refs_6_.1) | copy-start | bytes 7077892
  20.3 23.1 %copy-start.14 = (f32[1280]{0:T(1024)S(1)}, f32[1280]{0:T(1024)}, u32[]{:S(2)}) copy-start(f32[1280]{0:T(1024)} %gain_ref.6) | copy-start | bytes 15364
  23.5 25.7 %copy-start.21 = (bf16[256,1280]{1,0:T(8,128)(2,1)}, bf16[256,1280]{1,0:T(8,128)(2,1)S(1)}, u32[]{:S(2)}) copy-start(bf16[256,1280]{1,0:T(8,128)(2,1)S(1)} %collective-permute-done.2.refs_0_) | copy-start | bytes 1966084
  24.9 2.3 %collective-permute-start.3 = (bf16[4,32,2688]{2,1,0:T(8,128)(2,1)S(1)}, bf16[4,32,2688]{2,1,0:T(8,128)(2,1)S(1)}, u32[]{:S(2)}, u32[]{:S(2)}) collective-permute-start(bf16[4,32,2688]{2,1,0:T(8,128)(2,1)S(1)} %get-tuple-element.88), channel_id=1, source_target_pairs={{0,1},{1,0},{2,3},{3,2},{4,5},{5,4},{6,7},{7,6},{8,9},{9,8},{10,11... | collective-permute-start | bytes 2064392 | tf_op jit(solution)/shard_map/ppermute | solution.py:542
  25.0 17.4 %collective-permute-start.5 = (bf16[256,1280]{1,0:T(8,128)(2,1)}, bf16[256,1280]{1,0:T(8,128)(2,1)S(1)}, u32[]{:S(2)}, u32[]{:S(2)}) collective-permute-start(bf16[256,1280]{1,0:T(8,128)(2,1)} %get-tuple-element.84.refs_0_), channel_id=1, source_target_pairs={{0,2},{2,0},{1,3},{3,1},{4,6},{6,4},{5,7},{7,5},{8,10},{10,8},{9,1... | collective-permute-start | bytes 1966088 | tf_op jit(solution)/shard_map/ppermute | solution.py:542
  26.5 16.9 %collective-permute-start.4 = (bf16[256,1280]{1,0:T(8,128)(2,1)S(1)}, bf16[256,1280]{1,0:T(8,128)(2,1)}, u32[]{:S(2)}, u32[]{:S(2)}) collective-permute-start(bf16[256,1280]{1,0:T(8,128)(2,1)S(1)} %collective-permute-done.2.refs_0_), channel_id=1, source_target_pairs={{0,12},{4,0},{8,4},{12,8},{1,13},{5,1},{9,5},{13,9},{2,14},{6,2},{... | collective-permute-start | bytes 1966088 | tf_op jit(solution)/shard_map/ppermute | solution.py:542
  43.5 1.1 copy-start.11
  49.3 1.1 copy-start.6
  50.3 0.8 copy-start.19
  51.2 0.9 copy-start.23
  52.0 31.7 %collective-permute-start.6 = (bf16[256,2688]{1,0:T(8,128)(2,1)}, bf16[256,2688]{1,0:T(8,128)(2,1)}, u32[]{:S(2)}, u32[]{:S(2)}) collective-permute-start(bf16[256,2688]{1,0:T(8,128)(2,1)} %get-tuple-element.96.refs_0_), channel_id=1, source_target_pairs={{0,2},{2,0},{1,3},{3,1},{4,6},{6,4},{5,7},{7,5},{8,10},{10,8},{9,1... | collective-permute-start | bytes 4128776 | tf_op jit(solution)/shard_map/ppermute | solution.py:542
  52.6 33.7 %collective-permute-start.7 = (bf16[2,32,2688]{2,1,0:T(8,128)(2,1)}, bf16[2,32,2688]{2,1,0:T(8,128)(2,1)S(1)}, u32[]{:S(2)}, u32[]{:S(2)}) collective-permute-start(bf16[2,32,2688]{2,1,0:T(8,128)(2,1)} %get-tuple-element.98), channel_id=1, source_target_pairs={{0,4},{4,8},{8,12},{12,0},{1,5},{5,9},{9,13},{13,1},{2,6},{6,10},{... | collective-permute-start | bytes 1032200 | tf_op jit(solution)/shard_map/ppermute | solution.py:542
  52.6 33.7 %collective-permute-start.8 = (bf16[2,32,2688]{2,1,0:T(8,128)(2,1)}, bf16[2,32,2688]{2,1,0:T(8,128)(2,1)S(1)}, u32[]{:S(2)}, u32[]{:S(2)}) collective-permute-start(bf16[2,32,2688]{2,1,0:T(8,128)(2,1)} %get-tuple-element.99), channel_id=1, source_target_pairs={{0,8},{4,12},{8,0},{12,4},{1,9},{5,13},{9,1},{13,5},{2,10},{6,14},... | collective-permute-start | bytes 1032200 | tf_op jit(solution)/shard_map/ppermute | solution.py:542
  55.6 30.6 %collective-permute-start.9 = (bf16[2,32,2688]{2,1,0:T(8,128)(2,1)S(1)}, bf16[2,32,2688]{2,1,0:T(8,128)(2,1)S(1)}, u32[]{:S(2)}, u32[]{:S(2)}) collective-permute-start(bf16[2,32,2688]{2,1,0:T(8,128)(2,1)S(1)} %get-tuple-element.100), channel_id=1, source_target_pairs={{0,12},{4,0},{8,4},{12,8},{1,13},{5,1},{9,5},{13,9},{2,14},{6,2},{... | collective-permute-start | bytes 1032200 | tf_op jit(solution)/shard_map/ppermute | solution.py:542
  83.8 19.1 %collective-permute-start.11 = (bf16[256,1280]{1,0:T(8,128)(2,1)}, bf16[256,1280]{1,0:T(8,128)(2,1)S(1)}, u32[]{:S(2)}, u32[]{:S(2)}) collective-permute-start(bf16[256,1280]{1,0:T(8,128)(2,1)} %collective-permute-done.4.refs_1_), channel_id=1, source_target_pairs={{0,12},{4,0},{8,4},{12,8},{1,13},{5,1},{9,5},{13,9},{2,14},{6,2},{... | collective-permute-start | bytes 1966088 | tf_op jit(solution)/shard_map/ppermute | solution.py:542
  86.2 1.3 copy-start.4
  87.6 8.1 %copy-start.24 = (bf16[256,1280]{1,0:T(8,128)(2,1)S(1)}, bf16[256,1280]{1,0:T(8,128)(2,1)}, u32[]{:S(2)}) copy-start(bf16[256,1280]{1,0:T(8,128)(2,1)} %copy-done.23) | copy-start | bytes 1966084
  95.0 3.0 %copy-start.20 = (bf16[256,1344]{1,0:T(8,128)(2,1)S(1)}, bf16[256,1344]{1,0:T(8,128)(2,1)}, u32[]{:S(2)}) copy-start(bf16[256,1344]{1,0:T(8,128)(2,1)} %copy-done.19) | copy-start | bytes 2064388
  95.0 7.8 %collective-permute-start.10 = (bf16[128,1280]{1,0:T(8,128)(2,1)S(1)}, bf16[128,1280]{1,0:T(8,128)(2,1)S(1)}, u32[]{:S(2)}, u32[]{:S(2)}) collective-permute-start(bf16[128,1280]{1,0:T(8,128)(2,1)S(1)} %constant_dynamic-slice_fusion), channel_id=1, source_target_pairs={{0,2},{2,0},{1,3},{3,1},{4,6},{6,4},{5,7},{7,5},{8,10},{10,8},{9,1... | collective-permute-start | bytes 983048 | tf_op jit(solution)/shard_map/ppermute | solution.py:542
  98.0 5.4 %copy-start.7 = (f32[256,1280]{1,0:T(8,128)S(1)}, f32[256,1280]{1,0:T(8,128)}, u32[]{:S(2)}) copy-start(f32[256,1280]{1,0:T(8,128)} %copy-done.6) | copy-start | bytes 3932164
  98.0 24.1 %slice-start = ((s8[6553600]{0:T(1024)(128)(4,1)}), s8[4194304]{0:T(1024)(128)(4,1)S(1)}, s32[]{:S(2)}) async-start(s8[6553600]{0:T(1024)(128)(4,1)} %bitcast.8), calls=%async_computation | async-start | bytes 8388608
  102.9 10.7 %collective-permute-start.14 = (bf16[4,192,1344]{2,1,0:T(8,128)(2,1)S(1)}, bf16[4,192,1344]{2,1,0:T(8,128)(2,1)S(1)}, u32[]{:S(2)}, u32[]{:S(2)}) collective-permute-start(bf16[4,192,1344]{2,1,0:T(8,128)(2,1)S(1)} %get-tuple-element.113), channel_id=1, source_target_pairs={{0,1},{1,0},{2,3},{3,2},{4,5},{5,4},{6,7},{7,6},{8,9},{9,8},{10,11... | collective-permute-start | bytes 6193160 | tf_op jit(solution)/shard_map/ppermute | solution.py:542
  102.9 10.7 %collective-permute-start.15 = (bf16[4,160,1344]{2,1,0:T(8,128)(2,1)S(1)}, bf16[4,160,1344]{2,1,0:T(8,128)(2,1)S(1)}, u32[]{:S(2)}, u32[]{:S(2)}) collective-permute-start(bf16[4,160,1344]{2,1,0:T(8,128)(2,1)S(1)} %get-tuple-element.114), channel_id=1, source_target_pairs={{0,1},{1,0},{2,3},{3,2},{4,5},{5,4},{6,7},{7,6},{8,9},{9,8},{10,11... | collective-permute-start | bytes 5160968 | tf_op jit(solution)/shard_map/ppermute | solution.py:542
  103.8 9.7 %collective-permute-start.13 = (bf16[128,1280]{1,0:T(8,128)(2,1)S(1)}, bf16[128,1280]{1,0:T(8,128)(2,1)S(1)}, u32[]{:S(2)}, u32[]{:S(2)}) collective-permute-start(bf16[128,1280]{1,0:T(8,128)(2,1)S(1)} %shard_map.170.refs_0_), channel_id=1, source_target_pairs={{0,12},{4,0},{8,4},{12,8},{1,13},{5,1},{9,5},{13,9},{2,14},{6,2},{... | collective-permute-start | bytes 983048 | tf_op jit(solution)/shard_map/ppermute | solution.py:542
  104.3 12.9 %collective-permute-start.12 = (bf16[128,1280]{1,0:T(8,128)(2,1)S(1)}, bf16[128,1280]{1,0:T(8,128)(2,1)S(1)}, u32[]{:S(2)}, u32[]{:S(2)}) collective-permute-start(bf16[128,1280]{1,0:T(8,128)(2,1)S(1)} %shard_map.170.refs_0_), channel_id=1, source_target_pairs={{0,2},{2,0},{1,3},{3,1},{4,6},{6,4},{5,7},{7,5},{8,10},{10,8},{9,1... | collective-permute-start | bytes 983048 | tf_op jit(solution)/shard_map/ppermute | solution.py:542
  113.5 7.7 %copy-start.25 = (bf16[128,1280]{1,0:T(8,128)(2,1)}, bf16[128,1280]{1,0:T(8,128)(2,1)S(1)}, u32[]{:S(2)}) copy-start(bf16[128,1280]{1,0:T(8,128)(2,1)S(1)} %collective-permute-done.13.refs_2_) | copy-start | bytes 983044
  113.5 8.6 %slice-start.1 = ((s8[6553600]{0:T(1024)(128)(4,1)}), s8[2359296]{0:T(1024)(128)(4,1)S(1)}, s32[]{:S(2)}) async-start(s8[6553600]{0:T(1024)(128)(4,1)} %bitcast.8), calls=%async_computation.1 | async-start | bytes 4718592
  113.5 8.5 %copy-start.15 = (f32[1280]{0:T(1024)S(1)}, f32[1280]{0:T(1024)}, u32[]{:S(2)}) copy-start(f32[1280]{0:T(1024)} %gain_ref.7) | copy-start | bytes 15364
  113.6 8.5 %copy-start.22 = (bf16[256,1280]{1,0:T(8,128)(2,1)S(1)}, bf16[256,1280]{1,0:T(8,128)(2,1)}, u32[]{:S(2)}) copy-start(bf16[256,1280]{1,0:T(8,128)(2,1)} %copy-done.21) | copy-start | bytes 1966084
  115.7 1.0 copy-start.8
  116.7 21.6 %copy-start.10 = (bf16[352,1344]{1,0:T(8,128)(2,1)}, bf16[352,1344]{1,0:T(8,128)(2,1)S(1)}, u32[]{:S(2)}) copy-start(bf16[352,1344]{1,0:T(8,128)(2,1)S(1)} %get-tuple-element.131) | copy-start | bytes 2838532
  116.7 41.4 %collective-permute-start.20 = (bf16[352,1344]{1,0:T(8,128)(2,1)}, bf16[352,1344]{1,0:T(8,128)(2,1)}, u32[]{:S(2)}, u32[]{:S(2)}) collective-permute-start(bf16[352,1344]{1,0:T(8,128)(2,1)} %get-tuple-element.129), channel_id=1, source_target_pairs={{0,4},{4,8},{8,12},{12,0},{1,5},{5,9},{9,13},{13,1},{2,6},{6,10},{... | collective-permute-start | bytes 2838536 | tf_op jit(solution)/shard_map/ppermute | solution.py:542
  117.2 0.7 copy-start.27
  118.0 29.9 %collective-permute-start.17 = (bf16[128,1280]{1,0:T(8,128)(2,1)S(1)}, bf16[128,1280]{1,0:T(8,128)(2,1)}, u32[]{:S(2)}, u32[]{:S(2)}) collective-permute-start(bf16[128,1280]{1,0:T(8,128)(2,1)S(1)} %collective-permute-done.13.refs_2_), channel_id=1, source_target_pairs={{0,12},{4,0},{8,4},{12,8},{1,13},{5,1},{9,5},{13,9},{2,14},{6,2},{... | collective-permute-start | bytes 983048 | tf_op jit(solution)/shard_map/ppermute | solution.py:542
  121.3 26.7 %collective-permute-start.16 = (bf16[128,1280]{1,0:T(8,128)(2,1)S(1)}, bf16[128,1280]{1,0:T(8,128)(2,1)S(1)}, u32[]{:S(2)}, u32[]{:S(2)}) collective-permute-start(bf16[128,1280]{1,0:T(8,128)(2,1)S(1)} %collective-permute-done.13.refs_2_), channel_id=1, source_target_pairs={{0,2},{2,0},{1,3},{3,1},{4,6},{6,4},{5,7},{7,5},{8,10},{10,8},{9,1... | collective-permute-start | bytes 983048 | tf_op jit(solution)/shard_map/ppermute | solution.py:542
  138.3 1.9 copy-start.31
  140.2 1.9 copy-start.32
  147.9 0.7 copy-start.29
  148.6 8.9 %collective-permute-start.19 = (bf16[128,1280]{1,0:T(8,128)(2,1)}, bf16[128,1280]{1,0:T(8,128)(2,1)}, u32[]{:S(2)}, u32[]{:S(2)}) collective-permute-start(bf16[128,1280]{1,0:T(8,128)(2,1)} %collective-permute-done.17.refs_4_), channel_id=1, source_target_pairs={{0,12},{4,0},{8,4},{12,8},{1,13},{5,1},{9,5},{13,9},{2,14},{6,2},{... | collective-permute-start | bytes 983048 | tf_op jit(solution)/shard_map/ppermute | solution.py:542
  150.2 8.0 %collective-permute-start.18 = (bf16[128,1280]{1,0:T(8,128)(2,1)}, bf16[128,1280]{1,0:T(8,128)(2,1)}, u32[]{:S(2)}, u32[]{:S(2)}) collective-permute-start(bf16[128,1280]{1,0:T(8,128)(2,1)} %collective-permute-done.17.refs_4_), channel_id=1, source_target_pairs={{0,2},{2,0},{1,3},{3,1},{4,6},{6,4},{5,7},{7,5},{8,10},{10,8},{9,1... | collective-permute-start | bytes 983048 | tf_op jit(solution)/shard_map/ppermute | solution.py:542
  151.3 11.2 %copy-start.35 = (bf16[256,1280]{1,0:T(8,128)(2,1)S(1)}, bf16[256,1280]{1,0:T(8,128)(2,1)}, u32[]{:S(2)}) copy-start(bf16[256,1280]{1,0:T(8,128)(2,1)} %get-tuple-element.136) | copy-start | bytes 1966084
  158.1 7.3 %collective-permute-start.22 = (bf16[128,1280]{1,0:T(8,128)(2,1)}, bf16[128,1280]{1,0:T(8,128)(2,1)S(1)}, u32[]{:S(2)}, u32[]{:S(2)}) collective-permute-start(bf16[128,1280]{1,0:T(8,128)(2,1)} %collective-permute-done.19.refs_6_), channel_id=1, source_target_pairs={{0,2},{2,0},{1,3},{3,1},{4,6},{6,4},{5,7},{7,5},{8,10},{10,8},{9,1... | collective-permute-start | bytes 983048 | tf_op jit(solution)/shard_map/ppermute | solution.py:542
  159.2 6.3 %copy-start.30 = (bf16[128,1280]{1,0:T(8,128)(2,1)S(1)}, bf16[128,1280]{1,0:T(8,128)(2,1)}, u32[]{:S(2)}) copy-start(bf16[128,1280]{1,0:T(8,128)(2,1)} %copy-done.29) | copy-start | bytes 983044
  161.0 4.5 %copy-start.17 = (bf16[256,2560]{1,0:T(8,128)(2,1)S(1)}, bf16[256,2560]{1,0:T(8,128)(2,1)}, u32[]{:S(2)}) copy-start(bf16[256,2560]{1,0:T(8,128)(2,1)} %get-tuple-element.138.refs_10_) | copy-start | bytes 3932164
  161.0 4.5 %copy-start.18 = (bf16[256,2560]{1,0:T(8,128)(2,1)S(1)}, bf16[256,2560]{1,0:T(8,128)(2,1)}, u32[]{:S(2)}) copy-start(bf16[256,2560]{1,0:T(8,128)(2,1)} %get-tuple-element.140.refs_12_) | copy-start | bytes 3932164
  161.0 4.5 %copy-start.26 = (bf16[128,1280]{1,0:T(8,128)(2,1)S(1)}, bf16[128,1280]{1,0:T(8,128)(2,1)}, u32[]{:S(2)}) copy-start(bf16[128,1280]{1,0:T(8,128)(2,1)} %copy-done.25) | copy-start | bytes 983044
  161.0 4.5 %copy-start.28 = (bf16[128,1280]{1,0:T(8,128)(2,1)S(1)}, bf16[128,1280]{1,0:T(8,128)(2,1)}, u32[]{:S(2)}) copy-start(bf16[128,1280]{1,0:T(8,128)(2,1)} %copy-done.27) | copy-start | bytes 983044
  161.0 23.4 %collective-permute-start.21 = (bf16[352,1344]{1,0:T(8,128)(2,1)S(1)}, bf16[352,1344]{1,0:T(8,128)(2,1)S(1)}, u32[]{:S(2)}, u32[]{:S(2)}) collective-permute-start(bf16[352,1344]{1,0:T(8,128)(2,1)S(1)} %add_convert_fusion.1), channel_id=1, source_target_pairs={{0,4},{4,8},{8,12},{12,0},{1,5},{5,9},{9,13},{13,1},{2,6},{6,10},{... | collective-permute-start | bytes 2838536 | tf_op jit(solution)/shard_map/ppermute | solution.py:542
  165.5 19.4 %copy-start.9 = (bf16[352,1344]{1,0:T(8,128)(2,1)S(1)}, bf16[352,1344]{1,0:T(8,128)(2,1)}, u32[]{:S(2)}) copy-start(bf16[352,1344]{1,0:T(8,128)(2,1)} %copy-done.8) | copy-start | bytes 2838532
  182.1 4.6 %copy-start.34 = (f32[160,2560]{1,0:T(8,128)S(1)}, f32[160,2560]{1,0:T(8,128)}, u32[]{:S(2)}) copy-start(f32[160,2560]{1,0:T(8,128)} %get-tuple-element.148) | copy-start | bytes 4915204
  184.4 2.3 %collective-permute-start.24 = (bf16[160,2560]{1,0:T(8,128)(2,1)S(1)}, bf16[160,2560]{1,0:T(8,128)(2,1)S(1)}, u32[]{:S(2)}, u32[]{:S(2)}) collective-permute-start(bf16[160,2560]{1,0:T(8,128)(2,1)S(1)} %get-tuple-element.149), channel_id=1, source_target_pairs={{0,1},{1,0},{2,3},{3,2},{4,5},{5,4},{6,7},{7,6},{8,9},{9,8},{10,11... | collective-permute-start | bytes 2457608 | tf_op jit(solution)/shard_map/ppermute | solution.py:542
  184.4 3.7 %collective-permute-start.25 = (bf16[160,2560]{1,0:T(8,128)(2,1)S(1)}, bf16[160,2560]{1,0:T(8,128)(2,1)S(1)}, u32[]{:S(2)}, u32[]{:S(2)}) collective-permute-start(bf16[160,2560]{1,0:T(8,128)(2,1)S(1)} %get-tuple-element.151), channel_id=1, source_target_pairs={{0,1},{1,0},{2,3},{3,2},{4,5},{5,4},{6,7},{7,6},{8,9},{9,8},{10,11... | collective-permute-start | bytes 2457608 | tf_op jit(solution)/shard_map/ppermute | solution.py:542
  185.2 2.9 %copy-start.33 = (f32[160,2560]{1,0:T(8,128)S(1)}, f32[160,2560]{1,0:T(8,128)}, u32[]{:S(2)}) copy-start(f32[160,2560]{1,0:T(8,128)} %get-tuple-element.150) | copy-start | bytes 4915204
  185.2 25.7 %collective-permute-start.23 = (bf16[352,1344]{1,0:T(8,128)(2,1)S(1)}, bf16[352,1344]{1,0:T(8,128)(2,1)S(1)}, u32[]{:S(2)}, u32[]{:S(2)}) collective-permute-start(bf16[352,1344]{1,0:T(8,128)(2,1)S(1)} %add_convert_fusion), channel_id=1, source_target_pairs={{0,4},{4,8},{8,12},{12,0},{1,5},{5,9},{9,13},{13,1},{2,6},{6,10},{... | collective-permute-start | bytes 2838536 | tf_op jit(solution)/shard_map/ppermute | solution.py:542
where the time goes:
time: 213 us; the launch traced here: 212 us
  waiting for transfers between devices  95.6 us (45%)
  Pallas kernels  69.9 us (33%)
  starting transfers between devices  28.8 us (14%)
  local copies, waits for them, and re-layouts  11.6 us (5%)
  other arithmetic  5.3 us (2%)
    ppermute x26, waiting for transfers between devices, shift(): lax.ppermute(values, axis, [(i, (i + by) % count) for i in range(count)])  95.6 us
    ppermute x26, starting transfers between devices, shift(): lax.ppermute(values, axis, [(i, (i + by) % count) for i in range(count)])  28.8 us
    pallas_call x1, Pallas kernels, mlp_back(): pl.pallas_call(kernel, in_specs=[pl.BlockSpec(memory_space=pltpu.SMEM)] +...  16.6 us
    pallas_call x1, Pallas kernels, mlp_hidden(): pl.pallas_call(kernel, in_specs=in_vmem(2 + count), out_specs=in_vmem(3),...  16.2 us
    pallas_call x1, Pallas kernels, mlp_forward(): pl.pallas_call(kernel, in_specs=in_vmem(2) + [pl.BlockSpec(memory_space=p...  12.4 us
    unnamed x76, local copies, waits for them, and re-layouts  11.6 us
    pallas_call x1, Pallas kernels, adaptors_back(): pl.pallas_call(kernel, in_specs=[pl.BlockSpec(memory_space=pltpu.SMEM)] +...  7.41 us
    pallas_call x2, Pallas kernels, gradient_blocks(): pl.pallas_call(kernel, in_specs=[pl.BlockSpec(memory_space=pltpu.SMEM)] +...  6.34 us
  transfers between devices with their start and end apart: 26, of which 13 were waited for; matrix products, arithmetic and copies ran while one was open for 3% of the time, Pallas kernels for 29%

commit v1 on v0

--- a/solution.py
+++ b/solution.py
@@ -654,12 +654,13 @@
         back = norm_back(stream, gain_out, addends_mp(part)[0].astype(jnp.float32)).astype(jnp.bfloat16)
 
     held_s = [back]
-    rows_in, got_b, got_a = tie(shift(back, "dp", -1), shift(theirs_b, "teach"), shift(theirs_a, "teach"))
+    rows_in = shift(back, "dp", -1)
+    got_b, got_a = shift(theirs_b, "teach"), shift(theirs_a, "teach")
+    held, *sums = chip_blocks(info, (mine_a, mine_b), (got_a, got_b))
     if two:
         swapped = [shift(back, "mp")]
-        swapped[0], rows_in = tie(swapped[0], rows_in)
+        swapped[0], rows_in, held = tie(swapped[0], rows_in, held)
     held_s.append(rows_in)
-    held, *sums = chip_blocks(info, (mine_a, mine_b), (got_a, got_b))
 
     def columns(values, at, count):
         return lax.dynamic_slice_in_dim(values, at * count, count, 1)

time: 213 us -> 210 us (0.986)
  waiting for transfers between devices: 95.6 us -> 93 us
    ppermute x26, waiting for transfers between devices: 95.6 us -> 93 us  [shift(): lax.ppermute(values, axis, [(i, (i + by) % count) for i in range(count)])]
  transfers between devices with their start and end apart: 26 -> 26, of which waited for: 13 -> 15; matrix products, arithmetic and copies ran while one was open for 3% -> 3% of each run, Pallas kernels for 29% -> 30%
where the time goes in v1:
time: 210 us
  waiting for transfers between devices  93 us (44%)
  Pallas kernels  70 us (33%)
  starting transfers between devices  28.6 us (14%)
  local copies, waits for them, and re-layouts  11.6 us (6%)
  other arithmetic  5.3 us (3%)
    ppermute x26, waiting for transfers between devices, shift(): lax.ppermute(values, axis, [(i, (i + by) % count) for i in range(count)])  93 us
    ppermute x26, starting transfers between devices, shift(): lax.ppermute(values, axis, [(i, (i + by) % count) for i in range(count)])  28.6 us
    pallas_call x1, Pallas kernels, mlp_back(): pl.pallas_call(kernel, in_specs=[pl.BlockSpec(memory_space=pltpu.SMEM)] +...  16.6 us
    pallas_call x1, Pallas kernels, mlp_hidden(): pl.pallas_call(kernel, in_specs=in_vmem(2 + count), out_specs=in_vmem(3),...  16.3 us
    pallas_call x1, Pallas kernels, mlp_forward(): pl.pallas_call(kernel, in_specs=in_vmem(2) + [pl.BlockSpec(memory_space=p...  12.4 us
    unnamed x76, local copies, waits for them, and re-layouts  11.6 us
    pallas_call x1, Pallas kernels, adaptors_back(): pl.pallas_call(kernel, in_specs=[pl.BlockSpec(memory_space=pltpu.SMEM)] +...  7.41 us
    pallas_call x2, Pallas kernels, gradient_blocks(): pl.pallas_call(kernel, in_specs=[pl.BlockSpec(memory_space=pltpu.SMEM)] +...  6.34 us
  transfers between devices with their start and end apart: 26, of which 15 were waited for; matrix products, arithmetic and copies ran while one was open for 3% of the time, Pallas kernels for 30%

profile of v1, /device:TPU:0, one launch (start us, length us, event | category | flops | bytes accessed | tf_op | source)
XLA Modules:
  0.0 209.6 jit_solution(14069279086177838479)
XLA Ops:
  0.6 5.1 %collective-permute-start.2 = (bf16[256,1280]{1,0:T(8,128)(2,1)}, bf16[256,1280]{1,0:T(8,128)(2,1)S(1)}, u32[]{:S(2)}, u32[]{:S(2)}) collective-permute-start(bf16[256,1280]{1,0:T(8,128)(2,1)} %bitcast.12), channel_id=1, source_target_pairs={{0,12},{4,0},{8,4},{12,8},{1,13},{5,1},{9,5},{13,9},{2,14},{6,2},{... | collective-permute-start | bytes 1966088 | tf_op jit(solution)/shard_map/ppermute | solution.py:542
  5.7 1.5 collective-permute-start.1
  7.2 0.5 collective-permute-start
  7.8 0.1 pad_add_fusion.info_ref
  7.9 12.4 %shard_map.163 = (bf16[256,1280]{1,0:T(8,128)(2,1)}, bf16[256,2560]{1,0:T(8,128)(2,1)}, bf16[256,2560]{1,0:T(8,128)(2,1)}, bf16[256,1280]{1,0:T(8,128)(2,1)}) custom-call(bf16[256,1280]{1,0:T(8,128)(2,1)} %bitcast.13, f32[1280]{0:T(1024)} %gain_ref.7, bf16[1280,2560]{1,0:T(8,128)(2,1)} %w_ref.1, bf16[2560,1280]{1,0:T(8,128)(2,1)} %refs_9_.3), custom_call_target="tpu_custom_call" | custom-call | flops 3355443200 | bytes 13107200 | tf_op jit(solution)/shard_map/pallas_call | solution.py:116
  20.3 3.2 %collective-permute-done.peer_d = bf16[8,32,768]{2,1,0:T(8,128)(2,1)S(1)} collective-permute-done((bf16[8,32,768]{2,1,0:T(8,128)(2,1)}, bf16[8,32,768]{2,1,0:T(8,128)(2,1)S(1)}, u32[]{:S(2)}, u32[]{:S(2)}) %collective-permute-start) | collective-permute-done | bytes 393248 | tf_op jit(solution)/shard_map/ppermute | solution.py:542
  23.6 1.3 shard_map.164
  25.0 1.6 collective-permute-start.5
  26.5 0.7 collective-permute-start.4
  27.2 0.9 shard_map.165
  28.1 14.2 %collective-permute-done.5.refs_1_ = bf16[256,1280]{1,0:T(8,128)(2,1)S(1)} collective-permute-done((bf16[256,1280]{1,0:T(8,128)(2,1)}, bf16[256,1280]{1,0:T(8,128)(2,1)S(1)}, u32[]{:S(2)}, u32[]{:S(2)}) %collective-permute-start.5) | collective-permute-done | bytes 655392 | tf_op jit(solution)/shard_map/ppermute | solution.py:542
  42.3 1.1 collective-permute-done.4.refs_1_
  43.5 1.1 copy-done.11
  44.6 4.7 %shard_map.166 = (f32[256,1280]{1,0:T(8,128)S(1)}, bf16[256,1280]{1,0:T(8,128)(2,1)S(1)}, bf16[256,1344]{1,0:T(8,128)(2,1)S(1)}, bf16[256,1344]{1,0:T(8,128)(2,1)S(1)}, bf16[256,2688]{1,0:T(8,128)(2,1)}) custom-call(bf16[256,1280]{1,0:T(8,128)(2,1)S(1)} %bitcast.14, f32[1280]{0:T(1024)S(1)} %copy-done.14, bf16[1280,768]{1,0:T(8,128)(2,1)S(1)} %copy-done.1, ...), custom_call_target="tpu_custom_call" | custom-call | flops 1824522240 | bytes 7127040 | tf_op jit(solution)/shard_map/pallas_call | solution.py:393
  49.3 1.1 copy-done.6
  50.3 0.8 copy-done.19
  51.2 0.8 copy-done.23
  52.0 0.5 collective-permute-start.6
  52.6 3.0 %collective-permute-start.8 = (bf16[2,32,2688]{2,1,0:T(8,128)(2,1)}, bf16[2,32,2688]{2,1,0:T(8,128)(2,1)S(1)}, u32[]{:S(2)}, u32[]{:S(2)}) collective-permute-start(bf16[2,32,2688]{2,1,0:T(8,128)(2,1)} %get-tuple-element.97), channel_id=1, source_target_pairs={{0,8},{4,12},{8,0},{12,4},{1,9},{5,13},{9,1},{13,5},{2,10},{6,14},... | collective-permute-start | bytes 1032200 | tf_op jit(solution)/shard_map/ppermute | solution.py:542
  55.6 0.8 collective-permute-start.9
  56.4 27.4 %collective-permute-done.6.refs_1_ = bf16[256,2688]{1,0:T(8,128)(2,1)} collective-permute-done((bf16[256,2688]{1,0:T(8,128)(2,1)}, bf16[256,2688]{1,0:T(8,128)(2,1)}, u32[]{:S(2)}, u32[]{:S(2)}) %collective-permute-start.6) | collective-permute-done | bytes 1376288 | tf_op jit(solution)/shard_map/ppermute | solution.py:542
  83.8 2.5 %collective-permute-start.11 = (bf16[256,1280]{1,0:T(8,128)(2,1)}, bf16[256,1280]{1,0:T(8,128)(2,1)S(1)}, u32[]{:S(2)}, u32[]{:S(2)}) collective-permute-start(bf16[256,1280]{1,0:T(8,128)(2,1)} %collective-permute-done.4.refs_1_), channel_id=1, source_target_pairs={{0,12},{4,0},{8,4},{12,8},{1,13},{5,1},{9,5},{13,9},{2,14},{6,2},{... | collective-permute-start | bytes 1966088 | tf_op jit(solution)/shard_map/ppermute | solution.py:542
  86.3 1.3 copy-done.4
  87.6 7.4 %shard_map.167 = (bf16[256,1536]{1,0:T(8,128)(2,1)S(1)}, bf16[256,1152]{1,0:T(8,128)(2,1)S(1)}, bf16[256,1344]{1,0:T(8,128)(2,1)S(1)}, bf16[256,1280]{1,0:T(8,128)(2,1)S(1)}) custom-call(s32[3]{0:T(128)S(1)} %pad_add_fusion.info_ref, bf16[256,2688]{1,0:T(8,128)(2,1)} %get-tuple-element.94.refs_0_, bf16[256,2688]{1,0:T(8,128)(2,1)} %collective-permute-done.6.refs_1_, ...), custom_call_target="tpu_custom_call" | custom-call | flops 1824522240 | bytes 7127040 | tf_op jit(solution)/shard_map/pallas_call | solution.py:462
  95.0 0.6 collective-permute-start.10
  95.7 2.3 %shard_map.169 = (bf16[4,160,1344]{2,1,0:T(8,128)(2,1)S(1)}, bf16[4,160,1344]{2,1,0:T(8,128)(2,1)S(1)}) custom-call(s32[1]{0:T(128)} %bitcast.3.core_ref, bf16[256,1280]{1,0:T(8,128)(2,1)S(1)} %copy-done.24, bf16[256,1344]{1,0:T(8,128)(2,1)S(1)} %get-tuple-element.106.refs_1_), custom_call_target="tpu_custom_call" | custom-call | flops 880803840 | bytes 3440640 | tf_op jit(solution)/shard_map/pallas_call | solution.py:515
  98.0 4.0 %shard_map.168 = (bf16[4,192,1344]{2,1,0:T(8,128)(2,1)S(1)}, bf16[4,192,1344]{2,1,0:T(8,128)(2,1)S(1)}) custom-call(s32[1]{0:T(128)} %bitcast.3.core_ref, bf16[256,1536]{1,0:T(8,128)(2,1)S(1)} %get-tuple-element.101.refs_0_, bf16[256,1344]{1,0:T(8,128)(2,1)S(1)} %copy-done.20, bf16[256,1152]{1,0:T(8,128)(2,1)S(1)} %get-tuple-element.103.refs_2_, ...), custom_call_target="tpu_custom_call" | custom-call | flops 943718400 | bytes 4128768 | tf_op jit(solution)/shard_map/pallas_call | solution.py:515
  102.0 0.8 collective-permute-done.10.other_ref
  102.9 0.5 collective-permute-start.14
  103.4 0.5 shard_map.170.refs_0_
  103.8 0.5 collective-permute-start.13
  104.3 0.5 collective-permute-start.12
  104.9 4.8 %collective-permute-done.14.refs_2_ = bf16[4,160,1344]{2,1,0:T(8,128)(2,1)S(1)} collective-permute-done((bf16[4,160,1344]{2,1,0:T(8,128)(2,1)S(1)}, bf16[4,160,1344]{2,1,0:T(8,128)(2,1)S(1)}, u32[]{:S(2)}, u32[]{:S(2)}) %collective-permute-start.14) | collective-permute-done | bytes 1720352 | tf_op jit(solution)/shard_map/ppermute | solution.py:542
  109.7 2.2 %shard_map.171 = (bf16[352,1344]{1,0:T(8,128)(2,1)}, bf16[352,1344]{1,0:T(8,128)(2,1)S(1)}, bf16[352,1344]{1,0:T(8,128)(2,1)S(1)}, bf16[352,1344]{1,0:T(8,128)(2,1)S(1)}) custom-call(s32[3]{0:T(128)S(1)} %pad_add_fusion.info_ref, bf16[4,160,1344]{2,1,0:T(8,128)(2,1)S(1)} %get-tuple-element.111.refs_0_, bf16[4,192,1344]{2,1,0:T(8,128)(2,1)S(1)} %get-tuple-element.112.refs_1_, ...), custom_call_target="tpu_custom_call" | custom-call | flops 1892352 | bytes 11354112 | tf_op jit(solution)/shard_map/pallas_call | solution.py:177
  111.9 1.0 copy-done.8
  112.8 0.7 collective-permute-done.13.refs_2_
  113.5 0.1 collective-permute-done.12.refs_1_
  113.7 0.7 copy-done.27
  114.4 1.6 collective-permute-start.20
  116.0 2.2 %collective-permute-start.17 = (bf16[128,1280]{1,0:T(8,128)(2,1)S(1)}, bf16[128,1280]{1,0:T(8,128)(2,1)}, u32[]{:S(2)}, u32[]{:S(2)}) collective-permute-start(bf16[128,1280]{1,0:T(8,128)(2,1)S(1)} %collective-permute-done.13.refs_2_), channel_id=1, source_target_pairs={{0,12},{4,0},{8,4},{12,8},{1,13},{5,1},{9,5},{13,9},{2,14},{6,2},{... | collective-permute-start | bytes 983048 | tf_op jit(solution)/shard_map/ppermute | solution.py:542
  118.2 0.8 collective-permute-start.16
  119.0 16.3 %shard_map.172 = (bf16[768,1280]{1,0:T(8,128)(2,1)S(1)}, bf16[768,2560]{1,0:T(8,128)(2,1)S(1)}, bf16[768,2560]{1,0:T(8,128)(2,1)S(1)}) custom-call(f32[1280]{0:T(1024)S(1)} %copy-done.15, bf16[1280,2560]{1,0:T(8,128)(2,1)S(1)} %bitcast.9, bf16[256,1280]{1,0:T(8,128)(2,1)S(1)} %copy-done.22, bf16[256,1280]{1,0:T(8,128)(2,1)} %collective-permute-done.4.refs_1_, ...), custom_call_target="tpu_custom_call" | custom-call | flops 5033164800 | bytes 6553600 | tf_op jit(solution)/shard_map/pallas_call | solution.py:154
  135.3 1.9 copy-done.31
  137.2 1.9 copy-done.32
  139.2 6.3 %collective-permute-done.17.refs_4_ = bf16[128,1280]{1,0:T(8,128)(2,1)} collective-permute-done((bf16[128,1280]{1,0:T(8,128)(2,1)S(1)}, bf16[128,1280]{1,0:T(8,128)(2,1)}, u32[]{:S(2)}, u32[]{:S(2)}) %collective-permute-start.17) | collective-permute-done | bytes 327712 | tf_op jit(solution)/shard_map/ppermute | solution.py:542
  145.5 0.7 copy-done.29
  146.2 2.3 %collective-permute-start.19 = (bf16[128,1280]{1,0:T(8,128)(2,1)}, bf16[128,1280]{1,0:T(8,128)(2,1)}, u32[]{:S(2)}, u32[]{:S(2)}) collective-permute-start(bf16[128,1280]{1,0:T(8,128)(2,1)} %collective-permute-done.17.refs_4_), channel_id=1, source_target_pairs={{0,12},{4,0},{8,4},{12,8},{1,13},{5,1},{9,5},{13,9},{2,14},{6,2},{... | collective-permute-start | bytes 983048 | tf_op jit(solution)/shard_map/ppermute | solution.py:542
  148.5 1.1 collective-permute-start.18
  149.6 5.2 %collective-permute-done.19.refs_6_ = bf16[128,1280]{1,0:T(8,128)(2,1)} collective-permute-done((bf16[128,1280]{1,0:T(8,128)(2,1)}, bf16[128,1280]{1,0:T(8,128)(2,1)}, u32[]{:S(2)}, u32[]{:S(2)}) %collective-permute-start.19) | collective-permute-done | bytes 327712 | tf_op jit(solution)/shard_map/ppermute | solution.py:542
  154.8 1.6 collective-permute-done.18.refs_5_
  156.4 1.1 collective-permute-start.22
  157.5 1.8 add_convert_fusion.1
  159.3 0.6 collective-permute-start.21
  159.9 0.5 fusion.refs_8_
  160.4 3.2 %collective-permute-done.22.refs_7_ = bf16[128,1280]{1,0:T(8,128)(2,1)S(1)} collective-permute-done((bf16[128,1280]{1,0:T(8,128)(2,1)}, bf16[128,1280]{1,0:T(8,128)(2,1)S(1)}, u32[]{:S(2)}, u32[]{:S(2)}) %collective-permute-start.22) | collective-permute-done | bytes 327712 | tf_op jit(solution)/shard_map/ppermute | solution.py:542
  163.7 16.6 %shard_map.173 = (f32[160,2560]{1,0:T(8,128)}, f32[160,2560]{1,0:T(8,128)}, bf16[160,2560]{1,0:T(8,128)(2,1)S(1)}, bf16[160,2560]{1,0:T(8,128)(2,1)S(1)}) custom-call(s32[3]{0:T(128)S(1)} %pad_add_fusion.info_ref, bf16[128,1280]{1,0:T(8,128)(2,1)S(1)} %shard_map.170.refs_0_, bf16[128,1280]{1,0:T(8,128)(2,1)S(1)} %copy-done.28, ...), custom_call_target="tpu_custom_call" | custom-call | flops 10066329600 | bytes 22282240 | tf_op jit(solution)/shard_map/pallas_call | solution.py:285
  180.3 1.3 collective-permute-done.21
  181.7 0.5 collective-permute-start.25
  182.2 0.3 add_convert_fusion
  182.6 1.5 collective-permute-done.24
  184.0 1.3 convert_add_fusion.1
  185.4 1.3 convert_add_fusion
  186.7 21.5 %collective-permute-done.23.got_ref = bf16[352,1344]{1,0:T(8,128)(2,1)S(1)} collective-permute-done((bf16[352,1344]{1,0:T(8,128)(2,1)S(1)}, bf16[352,1344]{1,0:T(8,128)(2,1)S(1)}, u32[]{:S(2)}, u32[]{:S(2)}) %collective-permute-start.23) | collective-permute-done | bytes 946208 | tf_op jit(solution)/shard_map/ppermute | solution.py:542
  208.2 1.4 shard_map.174
  (84 shorter events, 0.4 us)
Async XLA Ops:
  0.6 22.9 %collective-permute-start.2 = (bf16[256,1280]{1,0:T(8,128)(2,1)}, bf16[256,1280]{1,0:T(8,128)(2,1)S(1)}, u32[]{:S(2)}, u32[]{:S(2)}) collective-permute-start(bf16[256,1280]{1,0:T(8,128)(2,1)} %bitcast.12), channel_id=1, source_target_pairs={{0,12},{4,0},{8,4},{12,8},{1,13},{5,1},{9,5},{13,9},{2,14},{6,2},{... | collective-permute-start | bytes 1966088 | tf_op jit(solution)/shard_map/ppermute | solution.py:542
  5.7 14.6 %collective-permute-start.1 = (bf16[8,32,576]{2,1,0:T(8,128)(2,1)}, bf16[8,32,576]{2,1,0:T(8,128)(2,1)S(1)}, u32[]{:S(2)}, u32[]{:S(2)}) collective-permute-start(bf16[8,32,576]{2,1,0:T(8,128)(2,1)} %own_s.1), channel_id=1, source_target_pairs={{0,2},{2,0},{1,3},{3,1},{4,6},{6,4},{5,7},{7,5},{8,10},{10,8},{9,1... | collective-permute-start | bytes 884744 | tf_op jit(solution)/shard_map/ppermute | solution.py:542
  7.2 16.3 %collective-permute-start = (bf16[8,32,768]{2,1,0:T(8,128)(2,1)}, bf16[8,32,768]{2,1,0:T(8,128)(2,1)S(1)}, u32[]{:S(2)}, u32[]{:S(2)}) collective-permute-start(bf16[8,32,768]{2,1,0:T(8,128)(2,1)} %own_d.1), channel_id=1, source_target_pairs={{0,2},{2,0},{1,3},{3,1},{4,6},{6,4},{5,7},{7,5},{8,10},{10,8},{9,1... | collective-permute-start | bytes 1179656 | tf_op jit(solution)/shard_map/ppermute | solution.py:542
  7.8 15.7 %copy-start.12 = (bf16[8,32,768]{2,1,0:T(8,128)(2,1)S(1)}, bf16[8,32,768]{2,1,0:T(8,128)(2,1)}, u32[]{:S(2)}) copy-start(bf16[8,32,768]{2,1,0:T(8,128)(2,1)} %own_d.1) | copy-start | bytes 1179652
  7.8 15.7 %copy-start.13 = (bf16[8,32,576]{2,1,0:T(8,128)(2,1)S(1)}, bf16[8,32,576]{2,1,0:T(8,128)(2,1)}, u32[]{:S(2)}) copy-start(bf16[8,32,576]{2,1,0:T(8,128)(2,1)} %own_s.1) | copy-start | bytes 884740
  7.8 15.7 %copy-start.16 = (s32[8]{0:T(128)S(1)}, s32[8]{0:T(128)}, u32[]{:S(2)}) copy-start(s32[8]{0:T(128)} %owner_ref.1) | copy-start | bytes 100
  7.8 35.6 %copy-start.1 = (bf16[1280,768]{1,0:T(8,128)(2,1)S(1)}, bf16[1280,768]{1,0:T(8,128)(2,1)}, u32[]{:S(2)}) copy-start(bf16[1280,768]{1,0:T(8,128)(2,1)} %refs_9_.2) | copy-start | bytes 5898244
  7.8 35.6 %copy-start.2 = (bf16[1280,576]{0,1:T(8,128)(2,1)S(1)}, bf16[1280,576]{0,1:T(8,128)(2,1)}, u32[]{:S(2)}) copy-start(bf16[1280,576]{0,1:T(8,128)(2,1)} %param.19) | copy-start | bytes 4423684
  7.9 35.6 %copy-start.3 = (bf16[576,1152]{1,0:T(8,128)(2,1)S(1)}, bf16[576,1152]{1,0:T(8,128)(2,1)}, u32[]{:S(2)}) copy-start(bf16[576,1152]{1,0:T(8,128)(2,1)} %refs_7_.1) | copy-start | bytes 3981316
  7.9 35.6 %copy-start.5 = (bf16[1,256,1280]{2,1,0:T(8,128)(2,1)S(1)}, bf16[1,256,1280]{2,1,0:T(8,128)(2,1)}, u32[]{:S(2)}) copy-start(bf16[1,256,1280]{2,1,0:T(8,128)(2,1)} %param.12) | copy-start | bytes 1966084
  20.3 23.1 %copy-start = (bf16[768,1536]{1,0:T(8,128)(2,1)S(1)}, bf16[768,1536]{1,0:T(8,128)(2,1)}, u32[]{:S(2)}) copy-start(bf16[768,1536]{1,0:T(8,128)(2,1)} %refs_6_.1) | copy-start | bytes 7077892
  20.3 23.1 %copy-start.14 = (f32[1280]{0:T(1024)S(1)}, f32[1280]{0:T(1024)}, u32[]{:S(2)}) copy-start(f32[1280]{0:T(1024)} %gain_ref.6) | copy-start | bytes 15364
  23.5 25.7 %copy-start.21 = (bf16[256,1280]{1,0:T(8,128)(2,1)}, bf16[256,1280]{1,0:T(8,128)(2,1)S(1)}, u32[]{:S(2)}) copy-start(bf16[256,1280]{1,0:T(8,128)(2,1)S(1)} %collective-permute-done.2.refs_0_) | copy-start | bytes 1966084
  24.9 2.3 %collective-permute-start.3 = (bf16[4,32,2688]{2,1,0:T(8,128)(2,1)S(1)}, bf16[4,32,2688]{2,1,0:T(8,128)(2,1)S(1)}, u32[]{:S(2)}, u32[]{:S(2)}) collective-permute-start(bf16[4,32,2688]{2,1,0:T(8,128)(2,1)S(1)} %get-tuple-element.86), channel_id=1, source_target_pairs={{0,1},{1,0},{2,3},{3,2},{4,5},{5,4},{6,7},{7,6},{8,9},{9,8},{10,11... | collective-permute-start | bytes 2064392 | tf_op jit(solution)/shard_map/ppermute | solution.py:542
  25.0 17.4 %collective-permute-start.5 = (bf16[256,1280]{1,0:T(8,128)(2,1)}, bf16[256,1280]{1,0:T(8,128)(2,1)S(1)}, u32[]{:S(2)}, u32[]{:S(2)}) collective-permute-start(bf16[256,1280]{1,0:T(8,128)(2,1)} %get-tuple-element.82.refs_0_), channel_id=1, source_target_pairs={{0,2},{2,0},{1,3},{3,1},{4,6},{6,4},{5,7},{7,5},{8,10},{10,8},{9,1... | collective-permute-start | bytes 1966088 | tf_op jit(solution)/shard_map/ppermute | solution.py:542
  26.5 16.9 %collective-permute-start.4 = (bf16[256,1280]{1,0:T(8,128)(2,1)S(1)}, bf16[256,1280]{1,0:T(8,128)(2,1)}, u32[]{:S(2)}, u32[]{:S(2)}) collective-permute-start(bf16[256,1280]{1,0:T(8,128)(2,1)S(1)} %collective-permute-done.2.refs_0_), channel_id=1, source_target_pairs={{0,12},{4,0},{8,4},{12,8},{1,13},{5,1},{9,5},{13,9},{2,14},{6,2},{... | collective-permute-start | bytes 1966088 | tf_op jit(solution)/shard_map/ppermute | solution.py:542
  43.5 1.1 copy-start.11
  49.3 1.1 copy-start.6
  50.3 0.8 copy-start.19
  51.2 0.9 copy-start.23
  52.0 31.7 %collective-permute-start.6 = (bf16[256,2688]{1,0:T(8,128)(2,1)}, bf16[256,2688]{1,0:T(8,128)(2,1)}, u32[]{:S(2)}, u32[]{:S(2)}) collective-permute-start(bf16[256,2688]{1,0:T(8,128)(2,1)} %get-tuple-element.94.refs_0_), channel_id=1, source_target_pairs={{0,2},{2,0},{1,3},{3,1},{4,6},{6,4},{5,7},{7,5},{8,10},{10,8},{9,1... | collective-permute-start | bytes 4128776 | tf_op jit(solution)/shard_map/ppermute | solution.py:542
  52.6 33.7 %collective-permute-start.7 = (bf16[2,32,2688]{2,1,0:T(8,128)(2,1)}, bf16[2,32,2688]{2,1,0:T(8,128)(2,1)S(1)}, u32[]{:S(2)}, u32[]{:S(2)}) collective-permute-start(bf16[2,32,2688]{2,1,0:T(8,128)(2,1)} %get-tuple-element.96), channel_id=1, source_target_pairs={{0,4},{4,8},{8,12},{12,0},{1,5},{5,9},{9,13},{13,1},{2,6},{6,10},{... | collective-permute-start | bytes 1032200 | tf_op jit(solution)/shard_map/ppermute | solution.py:542
  52.6 33.7 %collective-permute-start.8 = (bf16[2,32,2688]{2,1,0:T(8,128)(2,1)}, bf16[2,32,2688]{2,1,0:T(8,128)(2,1)S(1)}, u32[]{:S(2)}, u32[]{:S(2)}) collective-permute-start(bf16[2,32,2688]{2,1,0:T(8,128)(2,1)} %get-tuple-element.97), channel_id=1, source_target_pairs={{0,8},{4,12},{8,0},{12,4},{1,9},{5,13},{9,1},{13,5},{2,10},{6,14},... | collective-permute-start | bytes 1032200 | tf_op jit(solution)/shard_map/ppermute | solution.py:542
  55.6 30.6 %collective-permute-start.9 = (bf16[2,32,2688]{2,1,0:T(8,128)(2,1)S(1)}, bf16[2,32,2688]{2,1,0:T(8,128)(2,1)S(1)}, u32[]{:S(2)}, u32[]{:S(2)}) collective-permute-start(bf16[2,32,2688]{2,1,0:T(8,128)(2,1)S(1)} %get-tuple-element.98), channel_id=1, source_target_pairs={{0,12},{4,0},{8,4},{12,8},{1,13},{5,1},{9,5},{13,9},{2,14},{6,2},{... | collective-permute-start | bytes 1032200 | tf_op jit(solution)/shard_map/ppermute | solution.py:542
  83.8 19.1 %collective-permute-start.11 = (bf16[256,1280]{1,0:T(8,128)(2,1)}, bf16[256,1280]{1,0:T(8,128)(2,1)S(1)}, u32[]{:S(2)}, u32[]{:S(2)}) collective-permute-start(bf16[256,1280]{1,0:T(8,128)(2,1)} %collective-permute-done.4.refs_1_), channel_id=1, source_target_pairs={{0,12},{4,0},{8,4},{12,8},{1,13},{5,1},{9,5},{13,9},{2,14},{6,2},{... | collective-permute-start | bytes 1966088 | tf_op jit(solution)/shard_map/ppermute | solution.py:542
  86.2 1.3 copy-start.4
  87.6 8.1 %copy-start.24 = (bf16[256,1280]{1,0:T(8,128)(2,1)S(1)}, bf16[256,1280]{1,0:T(8,128)(2,1)}, u32[]{:S(2)}) copy-start(bf16[256,1280]{1,0:T(8,128)(2,1)} %copy-done.23) | copy-start | bytes 1966084
  95.0 3.0 %copy-start.20 = (bf16[256,1344]{1,0:T(8,128)(2,1)S(1)}, bf16[256,1344]{1,0:T(8,128)(2,1)}, u32[]{:S(2)}) copy-start(bf16[256,1344]{1,0:T(8,128)(2,1)} %copy-done.19) | copy-start | bytes 2064388
  95.0 7.8 %collective-permute-start.10 = (bf16[128,1280]{1,0:T(8,128)(2,1)S(1)}, bf16[128,1280]{1,0:T(8,128)(2,1)S(1)}, u32[]{:S(2)}, u32[]{:S(2)}) collective-permute-start(bf16[128,1280]{1,0:T(8,128)(2,1)S(1)} %constant_dynamic-slice_fusion), channel_id=1, source_target_pairs={{0,2},{2,0},{1,3},{3,1},{4,6},{6,4},{5,7},{7,5},{8,10},{10,8},{9,1... | collective-permute-start | bytes 983048 | tf_op jit(solution)/shard_map/ppermute | solution.py:542
  98.0 5.4 %copy-start.7 = (f32[256,1280]{1,0:T(8,128)S(1)}, f32[256,1280]{1,0:T(8,128)}, u32[]{:S(2)}) copy-start(f32[256,1280]{1,0:T(8,128)} %copy-done.6) | copy-start | bytes 3932164
  98.0 21.0 %slice-start = ((s8[6553600]{0:T(1024)(128)(4,1)}), s8[4194304]{0:T(1024)(128)(4,1)S(1)}, s32[]{:S(2)}) async-start(s8[6553600]{0:T(1024)(128)(4,1)} %bitcast.8), calls=%async_computation | async-start | bytes 8388608
  102.9 6.8 %collective-permute-start.15 = (bf16[4,192,1344]{2,1,0:T(8,128)(2,1)S(1)}, bf16[4,192,1344]{2,1,0:T(8,128)(2,1)S(1)}, u32[]{:S(2)}, u32[]{:S(2)}) collective-permute-start(bf16[4,192,1344]{2,1,0:T(8,128)(2,1)S(1)} %get-tuple-element.114), channel_id=1, source_target_pairs={{0,1},{1,0},{2,3},{3,2},{4,5},{5,4},{6,7},{7,6},{8,9},{9,8},{10,11... | collective-permute-start | bytes 6193160 | tf_op jit(solution)/shard_map/ppermute | solution.py:542
  102.9 6.8 %collective-permute-start.14 = (bf16[4,160,1344]{2,1,0:T(8,128)(2,1)S(1)}, bf16[4,160,1344]{2,1,0:T(8,128)(2,1)S(1)}, u32[]{:S(2)}, u32[]{:S(2)}) collective-permute-start(bf16[4,160,1344]{2,1,0:T(8,128)(2,1)S(1)} %get-tuple-element.113), channel_id=1, source_target_pairs={{0,1},{1,0},{2,3},{3,2},{4,5},{5,4},{6,7},{7,6},{8,9},{9,8},{10,11... | collective-permute-start | bytes 5160968 | tf_op jit(solution)/shard_map/ppermute | solution.py:542
  103.8 9.7 %collective-permute-start.13 = (bf16[128,1280]{1,0:T(8,128)(2,1)S(1)}, bf16[128,1280]{1,0:T(8,128)(2,1)S(1)}, u32[]{:S(2)}, u32[]{:S(2)}) collective-permute-start(bf16[128,1280]{1,0:T(8,128)(2,1)S(1)} %shard_map.170.refs_0_), channel_id=1, source_target_pairs={{0,12},{4,0},{8,4},{12,8},{1,13},{5,1},{9,5},{13,9},{2,14},{6,2},{... | collective-permute-start | bytes 983048 | tf_op jit(solution)/shard_map/ppermute | solution.py:542
  104.3 9.3 %collective-permute-start.12 = (bf16[128,1280]{1,0:T(8,128)(2,1)S(1)}, bf16[128,1280]{1,0:T(8,128)(2,1)S(1)}, u32[]{:S(2)}, u32[]{:S(2)}) collective-permute-start(bf16[128,1280]{1,0:T(8,128)(2,1)S(1)} %shard_map.170.refs_0_), channel_id=1, source_target_pairs={{0,2},{2,0},{1,3},{3,1},{4,6},{6,4},{5,7},{7,5},{8,10},{10,8},{9,1... | collective-permute-start | bytes 983048 | tf_op jit(solution)/shard_map/ppermute | solution.py:542
  109.7 9.3 %slice-start.1 = ((s8[6553600]{0:T(1024)(128)(4,1)}), s8[2359296]{0:T(1024)(128)(4,1)S(1)}, s32[]{:S(2)}) async-start(s8[6553600]{0:T(1024)(128)(4,1)} %bitcast.8), calls=%async_computation.1 | async-start | bytes 4718592
  109.7 9.3 %copy-start.15 = (f32[1280]{0:T(1024)S(1)}, f32[1280]{0:T(1024)}, u32[]{:S(2)}) copy-start(f32[1280]{0:T(1024)} %gain_ref.7) | copy-start | bytes 15364
  109.7 9.3 %copy-start.22 = (bf16[256,1280]{1,0:T(8,128)(2,1)S(1)}, bf16[256,1280]{1,0:T(8,128)(2,1)}, u32[]{:S(2)}) copy-start(bf16[256,1280]{1,0:T(8,128)(2,1)} %copy-done.21) | copy-start | bytes 1966084
  111.9 1.0 copy-start.8
  112.8 22.4 %copy-start.10 = (bf16[352,1344]{1,0:T(8,128)(2,1)}, bf16[352,1344]{1,0:T(8,128)(2,1)S(1)}, u32[]{:S(2)}) copy-start(bf16[352,1344]{1,0:T(8,128)(2,1)S(1)} %get-tuple-element.127) | copy-start | bytes 2838532
  113.5 21.8 %copy-start.25 = (bf16[128,1280]{1,0:T(8,128)(2,1)}, bf16[128,1280]{1,0:T(8,128)(2,1)S(1)}, u32[]{:S(2)}) copy-start(bf16[128,1280]{1,0:T(8,128)(2,1)S(1)} %collective-permute-done.13.refs_2_) | copy-start | bytes 983044
  113.7 0.7 copy-start.27
  114.4 42.0 %collective-permute-start.20 = (bf16[352,1344]{1,0:T(8,128)(2,1)}, bf16[352,1344]{1,0:T(8,128)(2,1)}, u32[]{:S(2)}, u32[]{:S(2)}) collective-permute-start(bf16[352,1344]{1,0:T(8,128)(2,1)} %get-tuple-element.125), channel_id=1, source_target_pairs={{0,4},{4,8},{8,12},{12,0},{1,5},{5,9},{9,13},{13,1},{2,6},{6,10},{... | collective-permute-start | bytes 2838536 | tf_op jit(solution)/shard_map/ppermute | solution.py:542
  116.0 29.5 %collective-permute-start.17 = (bf16[128,1280]{1,0:T(8,128)(2,1)S(1)}, bf16[128,1280]{1,0:T(8,128)(2,1)}, u32[]{:S(2)}, u32[]{:S(2)}) collective-permute-start(bf16[128,1280]{1,0:T(8,128)(2,1)S(1)} %collective-permute-done.13.refs_2_), channel_id=1, source_target_pairs={{0,12},{4,0},{8,4},{12,8},{1,13},{5,1},{9,5},{13,9},{2,14},{6,2},{... | collective-permute-start | bytes 983048 | tf_op jit(solution)/shard_map/ppermute | solution.py:542
  118.2 27.3 %collective-permute-start.16 = (bf16[128,1280]{1,0:T(8,128)(2,1)S(1)}, bf16[128,1280]{1,0:T(8,128)(2,1)S(1)}, u32[]{:S(2)}, u32[]{:S(2)}) collective-permute-start(bf16[128,1280]{1,0:T(8,128)(2,1)S(1)} %collective-permute-done.13.refs_2_), channel_id=1, source_target_pairs={{0,2},{2,0},{1,3},{3,1},{4,6},{6,4},{5,7},{7,5},{8,10},{10,8},{9,1... | collective-permute-start | bytes 983048 | tf_op jit(solution)/shard_map/ppermute | solution.py:542
  135.3 1.9 copy-start.31
  137.2 1.9 copy-start.32
  145.5 0.7 copy-start.29
  146.2 8.6 %collective-permute-start.19 = (bf16[128,1280]{1,0:T(8,128)(2,1)}, bf16[128,1280]{1,0:T(8,128)(2,1)}, u32[]{:S(2)}, u32[]{:S(2)}) collective-permute-start(bf16[128,1280]{1,0:T(8,128)(2,1)} %collective-permute-done.17.refs_4_), channel_id=1, source_target_pairs={{0,12},{4,0},{8,4},{12,8},{1,13},{5,1},{9,5},{13,9},{2,14},{6,2},{... | collective-permute-start | bytes 983048 | tf_op jit(solution)/shard_map/ppermute | solution.py:542
  148.5 7.9 %collective-permute-start.18 = (bf16[128,1280]{1,0:T(8,128)(2,1)}, bf16[128,1280]{1,0:T(8,128)(2,1)}, u32[]{:S(2)}, u32[]{:S(2)}) collective-permute-start(bf16[128,1280]{1,0:T(8,128)(2,1)} %collective-permute-done.17.refs_4_), channel_id=1, source_target_pairs={{0,2},{2,0},{1,3},{3,1},{4,6},{6,4},{5,7},{7,5},{8,10},{10,8},{9,1... | collective-permute-start | bytes 983048 | tf_op jit(solution)/shard_map/ppermute | solution.py:542
  149.6 10.3 %copy-start.35 = (bf16[256,1280]{1,0:T(8,128)(2,1)S(1)}, bf16[256,1280]{1,0:T(8,128)(2,1)}, u32[]{:S(2)}) copy-start(bf16[256,1280]{1,0:T(8,128)(2,1)} %get-tuple-element.132) | copy-start | bytes 1966084
  156.4 7.3 %collective-permute-start.22 = (bf16[128,1280]{1,0:T(8,128)(2,1)}, bf16[128,1280]{1,0:T(8,128)(2,1)S(1)}, u32[]{:S(2)}, u32[]{:S(2)}) collective-permute-start(bf16[128,1280]{1,0:T(8,128)(2,1)} %collective-permute-done.19.refs_6_), channel_id=1, source_target_pairs={{0,2},{2,0},{1,3},{3,1},{4,6},{6,4},{5,7},{7,5},{8,10},{10,8},{9,1... | collective-permute-start | bytes 983048 | tf_op jit(solution)/shard_map/ppermute | solution.py:542
  157.5 6.2 %copy-start.30 = (bf16[128,1280]{1,0:T(8,128)(2,1)S(1)}, bf16[128,1280]{1,0:T(8,128)(2,1)}, u32[]{:S(2)}) copy-start(bf16[128,1280]{1,0:T(8,128)(2,1)} %copy-done.29) | copy-start | bytes 983044
  159.3 4.4 %copy-start.17 = (bf16[256,2560]{1,0:T(8,128)(2,1)S(1)}, bf16[256,2560]{1,0:T(8,128)(2,1)}, u32[]{:S(2)}) copy-start(bf16[256,2560]{1,0:T(8,128)(2,1)} %get-tuple-element.134.refs_10_) | copy-start | bytes 3932164
  159.3 4.4 %copy-start.18 = (bf16[256,2560]{1,0:T(8,128)(2,1)S(1)}, bf16[256,2560]{1,0:T(8,128)(2,1)}, u32[]{:S(2)}) copy-start(bf16[256,2560]{1,0:T(8,128)(2,1)} %get-tuple-element.136.refs_12_) | copy-start | bytes 3932164
  159.3 4.4 %copy-start.26 = (bf16[128,1280]{1,0:T(8,128)(2,1)S(1)}, bf16[128,1280]{1,0:T(8,128)(2,1)}, u32[]{:S(2)}) copy-start(bf16[128,1280]{1,0:T(8,128)(2,1)} %copy-done.25) | copy-start | bytes 983044
  159.3 4.4 %copy-start.28 = (bf16[128,1280]{1,0:T(8,128)(2,1)S(1)}, bf16[128,1280]{1,0:T(8,128)(2,1)}, u32[]{:S(2)}) copy-start(bf16[128,1280]{1,0:T(8,128)(2,1)} %copy-done.27) | copy-start | bytes 983044
  159.3 22.4 %collective-permute-start.21 = (bf16[352,1344]{1,0:T(8,128)(2,1)S(1)}, bf16[352,1344]{1,0:T(8,128)(2,1)S(1)}, u32[]{:S(2)}, u32[]{:S(2)}) collective-permute-start(bf16[352,1344]{1,0:T(8,128)(2,1)S(1)} %add_convert_fusion.1), channel_id=1, source_target_pairs={{0,4},{4,8},{8,12},{12,0},{1,5},{5,9},{9,13},{13,1},{2,6},{6,10},{... | collective-permute-start | bytes 2838536 | tf_op jit(solution)/shard_map/ppermute | solution.py:542
  163.7 18.5 %copy-start.9 = (bf16[352,1344]{1,0:T(8,128)(2,1)S(1)}, bf16[352,1344]{1,0:T(8,128)(2,1)}, u32[]{:S(2)}) copy-start(bf16[352,1344]{1,0:T(8,128)(2,1)} %copy-done.8) | copy-start | bytes 2838532
  180.3 3.7 %copy-start.34 = (f32[160,2560]{1,0:T(8,128)S(1)}, f32[160,2560]{1,0:T(8,128)}, u32[]{:S(2)}) copy-start(f32[160,2560]{1,0:T(8,128)} %get-tuple-element.144) | copy-start | bytes 4915204
  181.7 2.3 %collective-permute-start.24 = (bf16[160,2560]{1,0:T(8,128)(2,1)S(1)}, bf16[160,2560]{1,0:T(8,128)(2,1)S(1)}, u32[]{:S(2)}, u32[]{:S(2)}) collective-permute-start(bf16[160,2560]{1,0:T(8,128)(2,1)S(1)} %get-tuple-element.145), channel_id=1, source_target_pairs={{0,1},{1,0},{2,3},{3,2},{4,5},{5,4},{6,7},{7,6},{8,9},{9,8},{10,11... | collective-permute-start | bytes 2457608 | tf_op jit(solution)/shard_map/ppermute | solution.py:542
  181.7 3.7 %collective-permute-start.25 = (bf16[160,2560]{1,0:T(8,128)(2,1)S(1)}, bf16[160,2560]{1,0:T(8,128)(2,1)S(1)}, u32[]{:S(2)}, u32[]{:S(2)}) collective-permute-start(bf16[160,2560]{1,0:T(8,128)(2,1)S(1)} %get-tuple-element.147), channel_id=1, source_target_pairs={{0,1},{1,0},{2,3},{3,2},{4,5},{5,4},{6,7},{7,6},{8,9},{9,8},{10,11... | collective-permute-start | bytes 2457608 | tf_op jit(solution)/shard_map/ppermute | solution.py:542
  182.5 2.9 %copy-start.33 = (f32[160,2560]{1,0:T(8,128)S(1)}, f32[160,2560]{1,0:T(8,128)}, u32[]{:S(2)}) copy-start(f32[160,2560]{1,0:T(8,128)} %get-tuple-element.146) | copy-start | bytes 4915204
  182.5 25.7 %collective-permute-start.23 = (bf16[352,1344]{1,0:T(8,128)(2,1)S(1)}, bf16[352,1344]{1,0:T(8,128)(2,1)S(1)}, u32[]{:S(2)}, u32[]{:S(2)}) collective-permute-start(bf16[352,1344]{1,0:T(8,128)(2,1)S(1)} %add_convert_fusion), channel_id=1, source_target_pairs={{0,4},{4,8},{8,12},{12,0},{1,5},{5,9},{9,13},{13,1},{2,6},{6,10},{... | collective-permute-start | bytes 2838536 | tf_op jit(solution)/shard_map/ppermute | solution.py:542
